TPU v7x, 128 devices: a whole 4x4x4 slice. The times are simulated.
128 devices in a mesh: lat: 32 (over y, x_hi, z), lon: 2 (over x_lo), section: 2 (over core).
Axes of the slice: x: 4 (x_hi: 2, x_lo: 2; x = x_hi * 2 + x_lo), y: 4, z: 4, core: 2. Of those that a mesh axis runs over, the one named last changes fastest.
Arguments:
- boundary: bfloat16 [2, 2, 2, 192, 24, 1024], P('section', None, None, 'lat', 'lon'), may hold values from -6 to 6
- tile_kinds: int32 [2, 32, 2], P('section', 'lat', 'lon'), may hold values from 0 to 3
- proj_in: bfloat16 [2, 1024, 3072], P('section'), may hold values from -0.1875 to 0.1875
- proj_out: bfloat16 [2, 1024, 1024], P('section'), may hold values from -0.375 to 0.375
- offset_bias: float32 [2, 16, 759], P('section'), may hold values from -4 to 250
Outputs:
- boundary_out: bfloat16 [2, 2, 2, 192, 24, 1024], P('section', None, None, 'lat', 'lon')
- weight_grads: float32 [2, 1024, 4096], P('section', ('lat', 'lon'))
- bias_grads: float32 [2, 16, 759], P('section')
All inputs are finite; a program needn't handle non-finite values.
Results may differ from a plain program's by a relative error of at most 0.025.
Values may be sent and summed in bfloat16 or wider, within the bound.
No kernel may reach another device: no remote copies, remote signals or barrier semaphores. Data moves between devices by JAX's collectives and lax.ppermute only.
A program may use at most 192 MiB of HBM per device.

v0:
```python
import functools

import jax
import jax.numpy as jnp
import numpy as np
from jax import lax
from jax.experimental import pallas as pl
from jax.experimental.pallas import tpu as pltpu
from jax.sharding import PartitionSpec as P

D = 1024
HEADS = 16
LEV = 2
MICRO = 2
WIN_LAT = 6
WIN_LON = 12
WT = 144
TOK = MICRO * WT
QT = TOK // 4
OFFSETS = 759
OPAD = 768
LEVEL_STEP = 253
ROW_STEP = 23
PAIRS = HEADS // 2
GROUP = 4
BIAS_ROWS = 16
NORM_EPS = 1e-05
MASKED = -1e30
BF = jnp.bfloat16
F32 = jnp.float32
VLIMIT = 58 * 1024 * 1024
SMALL = 24 * 1024 * 1024

HBM = pl.BlockSpec(memory_space=pltpu.HBM)
VMEM = pl.BlockSpec(memory_space=pltpu.VMEM)
SMEM = pl.BlockSpec(memory_space=pltpu.SMEM)


def constants():
    tok = np.arange(WT)
    row, col, lev = tok // 24, tok // 2 % 12, tok % 2
    onehot = np.zeros((256, 256), np.float32)
    onehot[tok, 128 * lev + 126 - 23 * row - col] = 1
    rows_differ = ((row < 3)[:, None] != (row < 3)[None, :]).astype(np.float32)
    cols_differ = ((col < 6)[:, None] != (col < 6)[None, :]).astype(np.float32)
    pick = np.zeros((4, QT, TOK), np.float32)
    for half_row in range(2):
        for half_col in range(2):
            at = 0
            for micro in range(MICRO):
                for level in range(LEV):
                    for r in range(3):
                        for c in range(6):
                            src = micro * WT + ((3 * half_row + r) * 12 + 6 * half_col + c) * 2 + level
                            pick[half_row * 2 + half_col, at, src] = 1
                            at += 1
    upper = np.concatenate([pick, np.zeros_like(pick)], axis=1).transpose(0, 2, 1)
    lower = np.concatenate([np.zeros_like(pick), pick], axis=1).transpose(0, 2, 1)
    return onehot, rows_differ, cols_differ, pick, upper, lower


ONEHOT, ROWS_DIFFER, COLS_DIFFER, PICK, UPPER, LOWER = constants()


def dot(a, b):
    return jnp.dot(a, b, preferred_element_type=F32)


def dot_nt(a, b):
    return lax.dot_general(a, b, (((1,), (1,)), ((), ())), preferred_element_type=F32)


def dot_tn(a, b):
    return lax.dot_general(a, b, (((0,), (0,)), ((), ())), preferred_element_type=F32)


def call(body, name, out_shape, in_specs, scratch, flops, nbytes, out_specs=None, limit=VLIMIT):
    if out_specs is None:
        out_specs = jax.tree.map(lambda _: VMEM, out_shape)
    return pl.pallas_call(
        body,
        out_shape=out_shape,
        in_specs=in_specs,
        out_specs=out_specs,
        scratch_shapes=scratch,
        compiler_params=pltpu.CompilerParams(vmem_limit_bytes=limit),
        cost_estimate=pl.CostEstimate(flops=flops, bytes_accessed=nbytes, transcendentals=0),
        name=name,
    )


def begin(src, dst, sem):
    copy = pltpu.make_async_copy(src, dst, sem)
    copy.start()
    return copy


def begin_weights(win, wout, win_v, wout_v, sem):
    made = []
    for i in range(6):
        cols = pl.ds(512 * i, 512)
        made.append(begin(win.at[:, cols], win_v.at[:, cols], sem.at[i]))
    made.append(begin(wout, wout_v, sem.at[6]))
    return made


def shape(*dims, dtype=BF):
    return jax.ShapeDtypeStruct(dims, dtype)


def load_block(x_ref, dst):
    dst[...] = x_ref[...].astype(F32).reshape(TOK, D)


def store_block(src, out_ref):
    out_ref[...] = src[...].astype(BF).reshape(TOK // 2, 2, D)


def insert(piece_refs, pick_ref):
    total = dot(pick_ref[0], piece_refs[0][...])
    for q in range(1, 4):
        total = total + dot(pick_ref[q], piece_refs[q][...])
    return total


def extract(first, second, pick_ref, out_refs):
    for q in range(4):
        out_refs[q][...] = jnp.concatenate([dot(pick_ref[q], first), dot(pick_ref[q], second)], axis=0).astype(BF)


def build_bias(kind, table_ref, oht_ref, rdiff, cdiff, out, tab, tops, mids, lows, tall, edge):
    tab[...] = jnp.zeros_like(tab)
    tab[:, :OFFSETS] = table_ref[...]
    for dl in range(3):
        for rq in range(6):
            for cq in range(12):
                start = LEVEL_STEP * dl + ROW_STEP * rq + cq
                at = ((dl * 6 + rq) * 12 + cq) * 16
                x = tab[:, start : start + 128]
                top = x.astype(BF)
                rest = x - top.astype(F32)
                mid = rest.astype(BF)
                tops[at : at + 16, :] = top
                mids[at : at + 16, :] = mid
                lows[at : at + 16, :] = (rest - mid.astype(F32)).astype(BF)
    for lq in range(2):
        for rq in range(6):
            one = ((1 + lq) * 6 + rq) * 192
            two = (lq * 6 + rq) * 192
            got = None
            for piece in (tops, mids, lows):
                x = jnp.concatenate([piece[one : one + 192, :], piece[two : two + 192, :]], axis=1)
                part = dot(x, oht_ref[...])
                got = part if got is None else got + part
            for cq in range(12):
                rows = pl.ds((rq * 12 + cq) * 2 + lq, 16, stride=WT)
                tall[rows, :] = got[cq * 16 : cq * 16 + 16, :128]
                edge[rows, :] = got[cq * 16 : cq * 16 + 16, 128:]
    split_rows = (kind[0] % 2).astype(F32)
    split_cols = (kind[0] // 2).astype(F32)
    closed = rdiff[...] * split_rows + cdiff[...] * split_cols > 0.0
    for h in range(HEADS):
        rows = slice(h * WT, h * WT + WT)
        out[rows, :128] = jnp.where(closed[:, :128], MASKED, tall[rows, :])
        out[rows, 128:] = jnp.where(closed[:, 128:], MASKED, edge[rows, : WT - 128])


def head_masks(scale):
    lane = lax.broadcasted_iota(jnp.int32, (1, 128), 1)
    low = jnp.where(lane < 64, scale, 0.0).astype(BF)
    high = jnp.where(lane >= 64, scale, 0.0).astype(BF)
    return low, high


def stacked(block, masks):
    return jnp.concatenate([block * masks[0], block * masks[1]], axis=0)


def norm_rows(xs, n_ref, at, count):
    x = xs[at : at + count, :]
    mean = jnp.mean(x, axis=-1, keepdims=True)
    centered = x - mean
    var = jnp.mean(centered * centered, axis=-1, keepdims=True)
    n_ref[at : at + count, :] = (centered * lax.rsqrt(var + NORM_EPS)).astype(BF)


def pair_lanes(p, base):
    return pl.ds(pl.multiple_of(base + p * 128, 128), 128)


def pair_rows(p):
    return pl.ds(pl.multiple_of(p * TOK, 8), TOK)


def forward_core(xs, win, wout, bias_ref, n_ref, c_ref, proj_ref, e_ref, inv_ref, out, weights, bias_ready, made):
    for at in range(0, TOK, 48):
        norm_rows(xs, n_ref, at, 48)
    made("n")
    for i in range(6):
        weights[i].wait()
        cols = slice(512 * i, 512 * i + 512)
        proj_ref[:, cols] = dot(n_ref[...], win[:, cols]).astype(BF)
    made("proj")
    bias_ready()

    @pl.loop(0, PAIRS, unroll=8)
    def _(p):
        eighth = head_masks(0.125)
        ones = head_masks(1.0)
        for w in range(MICRO):
            rows = slice(w * WT, w * WT + WT)
            qs = stacked(proj_ref[rows, pair_lanes(p, 0)], eighth)
            k = proj_ref[rows, pair_lanes(p, D)]
            v = proj_ref[rows, pair_lanes(p, 2 * D)]
            s = dot_nt(qs, k) + bias_ref[pair_rows(p), :]
            peak = jnp.max(s, axis=-1, keepdims=True)
            e = jnp.exp(s - peak).astype(BF)
            e_ref[pl.ds(pl.multiple_of((p * 2 + w) * TOK, 16), TOK), :] = e
            wide = [
                jnp.concatenate([v * one, jnp.broadcast_to(one, (WT, 128))], axis=1) for one in ones
            ]
            both = dot(e[:WT], wide[0]) + dot(e[WT:], wide[1])
            inv = 1.0 / both[:, 128:]
            c_ref[rows, pair_lanes(p, 0)] = (both[:, :128] * inv).astype(BF)
            inv_ref[pl.ds(pl.multiple_of((p * 2 + w) * WT, 16), WT), :] = inv.astype(BF)

    made("c")
    weights[6].wait()
    for c in range(0, D, 512):
        out[:, c : c + 512] = xs[:, c : c + 512] + dot(c_ref[...], wout[:, c : c + 512])


def ring_depth():
    lat = lax.axis_index("lat")
    return jnp.where(lax.axis_index("section") == 0, lax.rem(lat, GROUP), lax.div(lat, 2 * GROUP))


def backward_core(xs, go, win, wout, c_ref, proj_ref, e_ref, inv_ref, oh_ref, gctx, gp, bacc, edge, terms, out,
                  weights, ready, late_ref, late_sem):
    sent = []
    depth = ring_depth()
    part = [lax.rem(depth + step, GROUP) for step in range(GROUP)]
    for step in range(GROUP):
        cols = pl.ds(pl.multiple_of(256 * part[step], 128), 256)
        sent.append(begin(go.at[:, cols], late_ref[step].at[pl.ds(0, TOK), pl.ds(768, 256)], late_sem.at[step, 0]))
    if weights:
        weights[6].wait()
    for c in range(0, D, 256):
        gctx[:, c : c + 256] = dot_nt(go[...], wout[c : c + 256, :]).astype(BF)
    edge[...] = jnp.zeros_like(edge)
    ready()

    @pl.loop(0, PAIRS, unroll=4)
    def _(p):
        eighth = head_masks(0.125)
        ones = head_masks(1.0)
        full = jnp.ones((WT, 128), BF)
        total = None
        for w in range(MICRO):
            rows = slice(w * WT, w * WT + WT)
            qs = stacked(proj_ref[rows, pair_lanes(p, 0)], eighth)
            k = proj_ref[rows, pair_lanes(p, D)]
            v = proj_ref[rows, pair_lanes(p, 2 * D)]
            e = e_ref[pl.ds(pl.multiple_of((p * 2 + w) * TOK, 16), TOK), :]
            inv = inv_ref[pl.ds(pl.multiple_of((p * 2 + w) * WT, 16), WT), :]
            dc = (gctx[rows, pair_lanes(p, 0)].astype(F32) * inv.astype(F32)).astype(BF)
            dcs = stacked(dc, ones)
            along = -(dc.astype(F32) * c_ref[rows, pair_lanes(p, 0)].astype(F32))
            alongs = stacked(along.astype(BF), ones)
            slope = dot_nt(jnp.concatenate([dcs, alongs], axis=1), jnp.concatenate([v, full], axis=1))
            ds = e.astype(F32) * slope
            total = ds if total is None else total + ds
            dsb = ds.astype(BF)
            gp[rows, pair_lanes(p, 2 * D)] = dot_tn(e, dcs).astype(BF)
            gp[rows, pair_lanes(p, D)] = dot_tn(dsb, qs).astype(BF)
            ks = [k * one for one in eighth]
            gp[rows, pair_lanes(p, 0)] = (dot(dsb[:WT], ks[0]) + dot(dsb[WT:], ks[1])).astype(BF)
        bacc[pair_rows(p), :] = total[:, :128]
        edge[pair_rows(p), : WT - 128] = total[:, 128:]

    for step in range(GROUP):
        cols = pl.ds(pl.multiple_of(768 * part[step], 128), 768)
        sent.append(begin(gp.at[:, cols], late_ref[step].at[pl.ds(0, TOK), pl.ds(0, 768)], late_sem.at[step, 1]))

    acc = [jnp.zeros((BIAS_ROWS, 256), F32) for _ in range(3)]
    blank = jnp.zeros((BIAS_ROWS, 128), F32)
    for rq in range(6):
        got = []
        for lq in range(2):
            taken = [pl.ds((rq * 12 + cq) * 2 + lq, 16, stride=WT) for cq in range(12)]
            x = jnp.concatenate(
                [jnp.concatenate([ref[rows, :] for rows in taken], axis=0) for ref in (bacc, edge)], axis=1
            )
            top = x.astype(BF)
            low = (x - top.astype(F32)).astype(BF)
            got.append(dot(top, oh_ref[...]) + dot(low, oh_ref[...]))
        levels = [got[0][:, 128:], got[0][:, :128] + got[1][:, 128:], got[1][:, :128]]
        for dl in range(3):
            for cq in range(12):
                one = jnp.concatenate([levels[dl][cq * 16 : cq * 16 + 16], blank], axis=1)
                shift = ROW_STEP * rq + cq
                acc[dl] = acc[dl] + (pltpu.roll(one, shift, 1) if shift else one)
    folded = jnp.zeros((BIAS_ROWS, OPAD), F32)
    for dl in range(3):
        one = jnp.concatenate([acc[dl], jnp.zeros((BIAS_ROWS, OPAD - 256), F32)], axis=1)
        folded = folded + (pltpu.roll(one, LEVEL_STEP * dl, 1) if dl else one)
    terms[:, :OPAD] = folded.astype(BF)
    terms[:, OPAD:] = jnp.zeros((BIAS_ROWS, D - OPAD), BF)
    for step in range(GROUP):
        sent.append(begin(terms, late_ref[step].at[pl.ds(TOK, BIAS_ROWS), :], late_sem.at[step, 2]))

    if weights:
        for i in range(6):
            weights[i].wait()
    for c in range(0, D, 256):
        out[:, c : c + 256] = dot_nt(gp[...], win[c : c + 256, :]).astype(BF).astype(F32)
    for at in range(0, TOK, 48):
        rows = slice(at, at + 48)
        dn = out[rows, :]
        x = xs[rows, :]
        mean = jnp.mean(x, axis=-1, keepdims=True)
        centered = x - mean
        var = jnp.mean(centered * centered, axis=-1, keepdims=True)
        scale = lax.rsqrt(var + NORM_EPS)
        n = centered * scale
        along = jnp.mean(dn * n, axis=-1, keepdims=True)
        level = jnp.mean(dn, axis=-1, keepdims=True)
        dx = (scale * (dn - level - n * along)).astype(BF).astype(F32)
        out[rows, :] = go[rows, :].astype(F32) + dx
    return sent


def first_forward_body(kind, x_ref, cot_ref, table_ref, oht_ref, rdiff, cdiff, pick_ref, win, wout,
                       bias_out, n_out, c_out, proj_out, e_out, inv_out, p0, p1, p2, p3,
                       win_v, wout_v, bias_v, n, c, proj, e, inv, xs, out, tab, tops, mids, lows, tall, edge, wsem, osem):
    @pl.when(lax.axis_index("section") == 0)
    def _():
        begin_weights(win, wout, win_v, wout_v, wsem)

    build_bias(kind, table_ref, oht_ref, rdiff, cdiff, bias_v, tab, tops, mids, lows, tall, edge)
    bias_copy = begin(bias_v, bias_out, osem.at[4])

    @pl.when(lax.axis_index("section") == 0)
    def _():
        weights = [
            pltpu.make_async_copy(win.at[:, pl.ds(512 * i, 512)], win_v.at[:, pl.ds(512 * i, 512)], wsem.at[i])
            for i in range(6)
        ] + [pltpu.make_async_copy(wout, wout_v, wsem.at[6])]
        load_block(x_ref, xs)
        sent = []

        def made(name):
            if name == "n":
                sent.append(begin(n, n_out, osem.at[0]))
            if name == "proj":
                sent.append(begin(proj, proj_out, osem.at[1]))
            if name == "c":
                sent.append(begin(c, c_out, osem.at[2]))
                sent.append(begin(e, e_out, osem.at[3]))
                sent.append(begin(inv, inv_out, osem.at[5]))

        forward_core(xs, win_v, wout_v, bias_v, n, c, proj, e, inv, out, weights, lambda: None, made)
        load_block(cot_ref, xs)
        extract(out[...].astype(BF), xs[...].astype(BF), pick_ref, (p0, p1, p2, p3))
        for one in sent:
            one.wait()

    bias_copy.wait()


def second_body(r0, r1, r2, r3, pick_ref, upper_ref, lower_ref, oh_ref, na_ref, ca_ref, bias_ref, win, wout,
                nc_out, l0, l1, l2, l3, g0, g1, g2, g3,
                win_v, wout_v, c, proj, e, inv, xs, out, go, gctx, gp, bacc, edge, terms,
                wsem, isem, lsem, n, bias_v, second):
    @pl.when(lax.axis_index("section") == 1)
    def _():
        weights = begin_weights(win, wout, win_v, wout_v, wsem)
        bias_copy = begin(bias_ref, bias_v, isem.at[0])
        xs[...] = insert((r0, r1, r2, r3), upper_ref)
        sent = []

        def made(name):
            if name == "n":
                sent.append(begin(n, nc_out.at[:, pl.ds(0, D)], isem.at[1]))
            if name == "c":
                sent.append(begin(c, nc_out.at[:, pl.ds(D, D)], isem.at[2]))

        forward_core(xs, win_v, wout_v, bias_v, n, c, proj, e, inv, out, weights, bias_copy.wait, made)
        second[...] = out[...].astype(BF)
        go[...] = insert((r0, r1, r2, r3), lower_ref).astype(BF)
        sent += backward_core(xs, go, win_v, wout_v, c, proj, e, inv, oh_ref, gctx, gp, bacc, edge, terms,
                              out, None, lambda: None, (l0, l1, l2, l3), lsem)
        extract(out[...].astype(BF), second[...], pick_ref, (g0, g1, g2, g3))
        for one in sent:
            one.wait()

    @pl.when(lax.axis_index("section") == 0)
    def _():
        came = [begin(na_ref, n, isem.at[0]), begin(ca_ref, c, isem.at[1])]
        came[0].wait()
        gone = begin(n, nc_out.at[:, pl.ds(0, D)], isem.at[2])
        came[1].wait()
        begin(c, nc_out.at[:, pl.ds(D, D)], isem.at[3]).wait()
        gone.wait()


def first_backward_body(x_ref, g0, g1, g2, g3, upper_ref, oh_ref,
                        ca_ref, proj_ref, e_ref, inv_ref, win, wout, b0, b1, b2, b3,
                        l0, l1, l2, l3, out_ref,
                        win_v, wout_v, c, proj, e, inv, xs, out, go, gctx, gp, bacc, edge, terms,
                        wsem, isem, lsem, hold):
    @pl.when(lax.axis_index("section") == 0)
    def _():
        weights = [None] * 7
        weights[6] = begin(wout, wout_v, wsem.at[6])
        copies = [
            begin(proj_ref, proj, isem.at[0]),
            begin(e_ref, e, isem.at[1]),
            begin(inv_ref, inv, isem.at[2]),
            begin(ca_ref, c, isem.at[3]),
        ]
        for i in range(6):
            cols = pl.ds(512 * i, 512)
            weights[i] = begin(win.at[:, cols], win_v.at[:, cols], wsem.at[i])
        go[...] = insert((g0, g1, g2, g3), upper_ref).astype(BF)
        load_block(x_ref, xs)

        def ready():
            for one in copies:
                one.wait()

        sent = backward_core(xs, go, win_v, wout_v, c, proj, e, inv, oh_ref, gctx, gp, bacc, edge, terms,
                             out, weights, ready, (l0, l1, l2, l3), lsem)
        store_block(out, out_ref)
        for one in sent:
            one.wait()

    @pl.when(lax.axis_index("section") == 1)
    def _():
        came = [begin(src, hold.at[j], lsem.at[j, 0]) for j, src in enumerate((b0, b1, b2, b3))]
        gone = []
        for j, dst in enumerate((l0, l1, l2, l3)):
            came[j].wait()
            gone.append(begin(hold.at[j], dst, lsem.at[j, 1]))
        for one in gone:
            one.wait()


def second_result_body(g0, g1, g2, g3, lower_ref, out_ref, xs):
    @pl.when(lax.axis_index("section") == 0)
    def _():
        xs[...] = insert((g0, g1, g2, g3), lower_ref)
        store_block(xs, out_ref)


def flip_body(n0, n1, n2, n3, out_ref, held, sem):
    copies = [begin(src, held.at[pl.ds(TOK * j, TOK)], sem.at[j]) for j, src in enumerate((n0, n1, n2, n3))]
    for one in copies:
        one.wait()

    @pl.loop(0, 8)
    def _(i):
        at = pl.ds(pl.multiple_of(i * 256, 256), 256)
        out_ref[at, :] = held[:, at].T


def weight_body(nct, l0, l1, l2, l3, out, grads, made, tab, sem):
    late = (l0, l1, l2, l3)
    table = late[0][TOK:, :OPAD].astype(F32)
    for j in range(GROUP):
        grads[TOK * j : TOK * j + TOK, :] = late[j][:TOK, :]
        if j:
            table = table + late[j][TOK:, :OPAD].astype(F32)
    tab[...] = table
    depth = ring_depth()
    share = jnp.concatenate(
        [
            tab[:, pl.ds(pl.multiple_of(128 * depth, 128), 128)],
            tab[pl.ds(pl.multiple_of(8 * lax.rem(depth, 2), 8), 8), pl.ds(pl.multiple_of(512 + 128 * lax.div(depth, 2), 128), 128)],
        ],
        axis=0,
    ).astype(BF)
    made[:, 128:, :] = jnp.broadcast_to(share[None], (64, 24, 128))
    sent = []
    for rb in range(4):
        dst = slice(rb * 16, rb * 16 + 16)
        into = dot(nct[rb * 256 : rb * 256 + 256, :], grads[:, :768])
        for cb in range(6):
            made[dst, cb * 16 : cb * 16 + 16, :] = into[:, cb * 128 : cb * 128 + 128].astype(BF).reshape(16, 16, 128)
        outof = dot(nct[D + rb * 256 : D + rb * 256 + 256, :], grads[:, 768:])
        for cb in range(2):
            made[dst, 96 + cb * 16 : 112 + cb * 16, :] = outof[:, cb * 128 : cb * 128 + 128].astype(BF).reshape(16, 16, 128)
        sent.append(begin(made.at[pl.ds(rb * 16, 16)], out.at[pl.ds(rb * 16, 16)], sem.at[rb]))
    for one in sent:
        one.wait()


def sum_body(in_ref, w_ref, b_ref, bias):
    def fill(place):
        for part in range(GROUP):
            total = None
            for i in range(4):
                for xh in range(2):
                    for xl in range(2):
                        y, z = place(part, i)
                        one = in_ref[((y * 2 + xh) * 4 + z) * 2 + xl].astype(F32)
                        total = one if total is None else total + one
            for cb in range(6):
                w_ref[:, part * 768 + cb * 128 : part * 768 + cb * 128 + 128] = total[cb * 16 : cb * 16 + 16]
            for cb in range(2):
                at = 3 * D + part * 256 + cb * 128
                w_ref[:, at : at + 128] = total[96 + cb * 16 : 112 + cb * 16]
            bias[:, part * 128 : part * 128 + 128] = total[128:144]
            at = 8 * (part % 2)
            bias[at : at + 8, 512 + 128 * (part // 2) : 640 + 128 * (part // 2)] = total[144:152]
        b_ref[...] = bias[:, :OFFSETS]

    @pl.when(lax.axis_index("section") == 0)
    def _():
        fill(lambda part, i: (i, part))

    @pl.when(lax.axis_index("section") == 1)
    def _():
        fill(lambda part, i: (part, i))


def per_device(boundary, tile_kinds, proj_in, proj_out, offset_bias):
    axes = ("lat", "lon", "section")
    nlat, nlon = lax.axis_size("lat"), lax.axis_size("lon")
    section = lax.axis_index("section")
    kind = tile_kinds.reshape(1)
    x = boundary.transpose(0, 1, 3, 4, 2, 5).reshape(TOK // 2, 2, D)
    win = proj_in[0]
    wout = proj_out[0]
    onehot = jnp.asarray(ONEHOT, BF)
    onehot_t = jnp.asarray(ONEHOT.T, BF)
    pick = jnp.asarray(PICK, BF)
    upper = jnp.asarray(UPPER, BF)
    lower = jnp.asarray(LOWER, BF)

    def flat(lat, lon, sec):
        return ((lat % nlat) * nlon + lon % nlon) * 2 + sec

    def roll_pairs(dl, dn, sec):
        return [(flat(i, j, sec), flat(i + dl, j + dn, 1 - sec)) for i in range(nlat) for j in range(nlon)]

    def cross(value, sec):
        return lax.ppermute(value, axes, roll_pairs(0, 0, sec))

    far_first = [(1, 1), (1, 0), (0, 1), (0, 0)]

    def forth(pieces):
        got = [None] * 4
        for dl, dn in far_first:
            piece = pieces[(1 - dl) * 2 + (1 - dn)]
            got[dl * 2 + dn] = lax.ppermute(piece, axes, roll_pairs(-dl, -dn, 0))
        return got

    def back(pieces):
        got = [None] * 4
        for dl, dn in far_first:
            got[(1 - dl) * 2 + (1 - dn)] = lax.ppermute(pieces[dl * 2 + dn], axes, roll_pairs(dl, dn, 1))
        return got

    def rings(axis, sec):
        made = {}
        for y in range(4):
            for x in range(4):
                for z in range(4):
                    key = {"x": (y, z), "y": (x, z), "z": (x, y)}[axis]
                    made.setdefault(key, []).append(flat((y * 2 + x // 2) * 4 + z, x % 2, sec))
        return [made[key] for key in sorted(made)]

    def gather(value, groups):
        return deal([value] * GROUP, groups)

    def deal(values, groups):
        return [values[0]] + [
            lax.ppermute(values[step], axes, [(g[m], g[(m + step) % GROUP]) for g in groups for m in range(GROUP)])
            for step in range(1, GROUP)
        ]

    quarter = [shape(2 * QT, D)] * 4
    block = shape(TOK // 2, 2, D)
    f32 = functools.partial(shape, dtype=F32)
    vf32 = lambda *dims: pltpu.VMEM(dims, F32)
    vbf = lambda *dims: pltpu.VMEM(dims, BF)
    dma = lambda *dims: pltpu.SemaphoreType.DMA(dims)
    wide = shape(TOK, 3 * D)
    whole = shape(TOK, D)
    exps = shape(PAIRS * MICRO * TOK, WT)
    invs = shape(PAIRS * MICRO * WT, 128)
    late_shape = [shape(TOK + BIAS_ROWS, D)] * GROUP
    weights_v = [vbf(D, 3 * D), vbf(D, D)]
    soft_v = [vbf(PAIRS * MICRO * TOK, WT), vbf(PAIRS * MICRO * WT, 128)]
    tall = [vf32(HEADS * WT, 128), vf32(HEADS * WT, 128)]
    pieces_v = [vbf(3 * 1152, 128)] * 3
    front_v = [vf32(HEADS * WT, WT), vbf(TOK, D), vbf(TOK, D), vbf(TOK, 3 * D)] + soft_v + [vf32(TOK, D), vf32(TOK, D)]
    back_v = (
        weights_v
        + [vbf(TOK, D), vbf(TOK, 3 * D)] + soft_v + [vf32(TOK, D), vf32(TOK, D)]
        + [vbf(TOK, D), vbf(TOK, D), vbf(TOK, 3 * D)]
        + tall
        + [vbf(BIAS_ROWS, D), dma(7), dma(4), dma(GROUP, 3)]
    )

    bias, n_a, c_a, proj_a, e_a, inv_a, *pieces = call(
        first_forward_body, "first_forward", [f32(HEADS * WT, WT), whole, whole, wide, exps, invs] + quarter,
        [SMEM] + [VMEM] * 7 + [HBM] * 2,
        weights_v + front_v + [vf32(HEADS, OPAD)] + pieces_v + tall + [dma(7), dma(6)],
        5_000_000_000, 20_000_000, [HBM] * 6 + [VMEM] * 4,
    )(kind, x, cross(x, 1), offset_bias[0], onehot_t, jnp.asarray(ROWS_DIFFER), jnp.asarray(COLS_DIFFER), pick, win, wout)
    received = forth(pieces)
    both, *pieces = call(
        second_body, "second_both", [shape(TOK, 2 * D)] + late_shape + quarter,
        [VMEM] * 8 + [HBM] * 5,
        back_v + [vbf(TOK, D), vf32(HEADS * WT, WT), vbf(TOK, D)], 12_000_000_000, 20_000_000, [HBM] * 5 + [VMEM] * 4,
    )(*received, pick, upper, lower, onehot, n_a, c_a, bias, win, wout)
    late_b, grads = pieces[:4], pieces[4:]
    grads = back(grads)
    grads, both = lax.optimization_barrier((grads, both))
    both = gather(both, rings("z", 0) + rings("y", 1))

    *late, grad_in = call(
        first_backward_body, "first_backward", late_shape + [block],
        [VMEM] * 7 + [HBM] * 10,
        back_v + [vbf(GROUP, TOK + BIAS_ROWS, D)], 8_000_000_000, 20_000_000, [HBM] * 4 + [VMEM],
    )(x, *grads, upper, onehot, c_a, proj_a, e_a, inv_a, win, wout, *late_b)
    late, grad_in, grads = lax.optimization_barrier((late, grad_in, grads))
    late = deal(late, rings("z", 0) + rings("y", 1))

    flipped = call(
        flip_body, "flip", shape(2 * D, GROUP * TOK), [HBM] * 4,
        [vbf(GROUP * TOK, 2 * D), dma(GROUP)], 10_000_000, 10_000_000, limit=SMALL,
    )(*both)
    second_out = call(
        second_result_body, "second_result", block, [VMEM] * 5, [vf32(TOK, D)], 170_000_000, 2_000_000, limit=SMALL,
    )(*grads, lower)

    terms = call(
        weight_body, "weight_terms", shape(64, 152, 128), [VMEM] * 5,
        [vbf(GROUP * TOK, D), vbf(64, 152, 128), vf32(HEADS, OPAD), dma(4)], 2_400_000_000, 10_000_000, HBM, limit=SMALL,
    )(flipped, *late)
    terms, second_out = lax.optimization_barrier((terms, cross(second_out, 0)))
    terms = lax.all_to_all(terms, ("lat", "lon"), 0, 0, tiled=True)
    result = jnp.where(section == 0, grad_in, second_out)
    result = result.reshape(1, MICRO, 6, 12, 2, D).transpose(0, 1, 4, 2, 3, 5)
    weights, table = call(
        sum_body, "sum_terms", [f32(16, 4 * D), f32(HEADS, OFFSETS)], [VMEM], [vf32(HEADS, OPAD)], 3_000_000, 3_000_000, limit=SMALL,
    )(terms)
    return (result, weights[None], table[None])


def solution(mesh):
    return jax.shard_map(
        per_device,
        mesh=mesh,
        in_specs=(
            P("section", None, None, "lat", "lon", None),
            P("section", "lat", "lon"),
            P("section", None, None),
            P("section", None, None),
            P("section", None, None),
        ),
        out_specs=(
            P("section", None, None, "lat", "lon", None),
            P("section", ("lat", "lon"), None),
            P("section", None, None),
        ),
        check_vma=False,
    )
```

profile of v0, /device:TPU:0, one launch (start us, length us, event | category | flops | bytes accessed | tf_op | source)
XLA Modules:
  0.0 157.4 jit_solution(11024010897396599149)
XLA Ops:
  0.6 1.3 collective-permute-start
  2.6 2.2 %collective-permute-done.cot_ref = bf16[144,2,1024]{2,1,0:T(2,128)(2,1)S(1)} collective-permute-done((bf16[144,2,1024]{2,1,0:T(2,128)(2,1)}, bf16[144,2,1024]{2,1,0:T(2,128)(2,1)S(1)}, u32[]{:S(2)}, u32[]{:S(2)}) %collective-permute-start) | collective-permute-done | bytes 589856 | tf_op jit(solution)/shard_map/ppermute | solution.py:548
  5.6 13.6 %first_forward.1 = (f32[2304,144]{1,0:T(8,128)}, bf16[288,1024]{1,0:T(8,128)(2,1)}, bf16[288,1024]{1,0:T(8,128)(2,1)}, bf16[288,3072]{1,0:T(8,128)(2,1)}, bf16[4...) custom-call(s32[1]{0:T(128)} %bitcast.15.kind, ...), custom_call_target="tpu_custom_call" | custom-call | flops 5000000000 | bytes 20000000 | tf_op jit(solution)/shard_map/first_forward/pallas_call | solution.py:607
  19.1 1.3 collective-permute-start.1
  20.5 1.3 collective-permute-start.2
  21.8 3.9 %collective-permute-start.3 = (bf16[144,1024]{1,0:T(8,128)(2,1)}, bf16[144,1024]{1,0:T(8,128)(2,1)S(1)}, u32[]{:S(2)}, u32[]{:S(2)}) collective-permute-start(bf16[144,1024]{1,0:T(8,128)(2,1)} %get-tuple-element.47), channel_id=1, source_target_pairs={{0,125},{2,127},{4,1},{6,3},{8,5},{10,7},{12,9},{14,11},{16,13},{1... | collective-permute-start | bytes 884744 | tf_op jit(solution)/shard_map/ppermute | solution.py:556
  25.7 1.3 collective-permute-start.4
  27.1 3.2 %collective-permute-done.3.r2 = bf16[144,1024]{1,0:T(8,128)(2,1)S(1)} collective-permute-done((bf16[144,1024]{1,0:T(8,128)(2,1)}, bf16[144,1024]{1,0:T(8,128)(2,1)S(1)}, u32[]{:S(2)}, u32[]{:S(2)}) %collective-permute-start.3) | collective-permute-done | bytes 294944 | tf_op jit(solution)/shard_map/ppermute | solution.py:556
  30.3 3.4 %collective-permute-done.4.r3 = bf16[144,1024]{1,0:T(8,128)(2,1)S(1)} collective-permute-done((bf16[144,1024]{1,0:T(8,128)(2,1)}, bf16[144,1024]{1,0:T(8,128)(2,1)S(1)}, u32[]{:S(2)}, u32[]{:S(2)}) %collective-permute-start.4) | collective-permute-done | bytes 294944 | tf_op jit(solution)/shard_map/ppermute | solution.py:556
  34.4 5.1 %second_both.1 = (bf16[288,2048]{1,0:T(8,128)(2,1)}, bf16[304,1024]{1,0:T(8,128)(2,1)}, bf16[304,1024]{1,0:T(8,128)(2,1)}, bf16[304,1024]{1,0:T(8,128)(2,1)}, bf...) custom-call(bf16[144,1024]{1,0:T(8,128)(2,1)} %copy-done.13, ...), custom_call_target="tpu_custom_call" | custom-call | flops 12000000000 | bytes 20000000 | tf_op jit(solution)/shard_map/second_both/pallas_call | solution.py:614
  39.5 1.3 collective-permute-start.5
  44.7 27.3 %collective-permute-done.5.g0 = bf16[144,1024]{1,0:T(8,128)(2,1)S(1)} collective-permute-done((bf16[144,1024]{1,0:T(8,128)(2,1)}, bf16[144,1024]{1,0:T(8,128)(2,1)S(1)}, u32[]{:S(2)}, u32[]{:S(2)}) %collective-permute-start.5) | collective-permute-done | bytes 294944 | tf_op jit(solution)/shard_map/ppermute | solution.py:562
  72.4 2.0 %collective-permute-start.9 = (bf16[288,2048]{1,0:T(8,128)(2,1)}, bf16[288,2048]{1,0:T(8,128)(2,1)S(1)}, u32[]{:S(2)}, u32[]{:S(2)}) collective-permute-start(bf16[288,2048]{1,0:T(8,128)(2,1)} %get-tuple-element.74.n0), channel_id=1, source_target_pairs={{0,4},{4,8},{8,12},{12,0},{32,36},{36,40},{40,44},{44,32},{64,68},... | collective-permute-start | bytes 3538952 | tf_op jit(solution)/shard_map/ppermute | solution.py:579
  74.4 16.6 %first_backward.1 = (bf16[304,1024]{1,0:T(8,128)(2,1)}, bf16[304,1024]{1,0:T(8,128)(2,1)}, bf16[304,1024]{1,0:T(8,128)(2,1)}, bf16[304,1024]{1,0:T(8,128)(2,1)}, bf16[144,2,1024]{2,1,0:T(2,128)(2,1)}) custom-call(bf16[144,2,1024]{2,1,0:T(2,128)(2,1)} %bitcast.26, bf16[144,1024]{1,0:T(8,128)(2,1)} %copy-done.3, bf16[144,1024]{1,0:T(8,128)(2,1)} %copy-done.5, ...), custom_call_target="tpu_custom_call" | custom-call | flops 8000000000 | bytes 20000000 | tf_op jit(solution)/shard_map/first_backward/pallas_call | solution.py:624
  91.1 1.5 collective-permute-start.12
  92.5 2.2 %collective-permute-start.13 = (bf16[304,1024]{1,0:T(8,128)(2,1)}, bf16[304,1024]{1,0:T(8,128)(2,1)S(1)}, u32[]{:S(2)}, u32[]{:S(2)}) collective-permute-start(bf16[304,1024]{1,0:T(8,128)(2,1)} %get-tuple-element.77), channel_id=1, source_target_pairs={{0,8},{4,12},{8,0},{12,4},{32,40},{36,44},{40,32},{44,36},{64,72},... | collective-permute-start | bytes 1867784 | tf_op jit(solution)/shard_map/ppermute | solution.py:579
  94.7 2.5 %collective-permute-start.14 = (bf16[304,1024]{1,0:T(8,128)(2,1)}, bf16[304,1024]{1,0:T(8,128)(2,1)S(1)}, u32[]{:S(2)}, u32[]{:S(2)}) collective-permute-start(bf16[304,1024]{1,0:T(8,128)(2,1)} %get-tuple-element.78), channel_id=1, source_target_pairs={{0,12},{4,0},{8,4},{12,8},{32,44},{36,32},{40,36},{44,40},{64,76},... | collective-permute-start | bytes 1867784 | tf_op jit(solution)/shard_map/ppermute | solution.py:579
  101.9 2.3 %collective-permute-start.15 = (bf16[144,2,1024]{2,1,0:T(2,128)(2,1)S(1)}, bf16[144,2,1024]{2,1,0:T(2,128)(2,1)}, u32[]{:S(2)}, u32[]{:S(2)}) collective-permute-start(bf16[144,2,1024]{2,1,0:T(2,128)(2,1)S(1)} %second_result.1), channel_id=1, source_target_pairs={{0,1},{2,3},{4,5},{6,7},{8,9},{10,11},{12,13},{14,15},{16,17},{18,... | collective-permute-start | bytes 1769480 | tf_op jit(solution)/shard_map/ppermute | solution.py:548
  104.1 2.7 %flip.1.nct = bf16[2048,1152]{1,0:T(8,128)(2,1)S(1)} custom-call(bf16[288,2048]{1,0:T(8,128)(2,1)S(1)} %copy-done, bf16[288,2048]{1,0:T(8,128)(2,1)S(1)} %collective-permute-done.9.n1, bf16[288,2048]{1,0:T(8,128)(2,1)S(1)} %collective-permute-done.10.n2, bf16[288,2048]{1,0:T(8,128)(2,1)S(1)} %collective-permute-done.11.n3), custom_call_target="tpu_custom_call" | custom-call | flops 10000000 | bytes 10000000 | tf_op jit(solution)/shard_map/flip/pallas_call | solution.py:632
  106.8 2.7 %collective-permute-done.12.l1 = bf16[304,1024]{1,0:T(8,128)(2,1)S(1)} collective-permute-done((bf16[304,1024]{1,0:T(8,128)(2,1)}, bf16[304,1024]{1,0:T(8,128)(2,1)S(1)}, u32[]{:S(2)}, u32[]{:S(2)}) %collective-permute-start.12) | collective-permute-done | bytes 622624 | tf_op jit(solution)/shard_map/ppermute | solution.py:579
  109.5 6.7 %collective-permute-done.13.l2 = bf16[304,1024]{1,0:T(8,128)(2,1)S(1)} collective-permute-done((bf16[304,1024]{1,0:T(8,128)(2,1)}, bf16[304,1024]{1,0:T(8,128)(2,1)S(1)}, u32[]{:S(2)}, u32[]{:S(2)}) %collective-permute-start.13) | collective-permute-done | bytes 622624 | tf_op jit(solution)/shard_map/ppermute | solution.py:579
  116.2 3.8 %weight_terms.1 = bf16[64,152,128]{2,1,0:T(8,128)(2,1)} custom-call(bf16[2048,1152]{1,0:T(8,128)(2,1)S(1)} %flip.1.nct, bf16[304,1024]{1,0:T(8,128)(2,1)S(1)} %copy-done.1, bf16[304,1024]{1,0:T(8,128)(2,1)S(1)} %collective-permute-done.12.l1, bf16[304,1024]{1,0:T(8,128)(2,1)S(1)} %collective-permute-done.13.l2, bf16[304,1024]{1,0:T(8,128)(2,1)S(1)} %collective-permute-done.14.l3), custom_call_target="tpu_custom_call" | custom-call | flops 2400000000 | bytes 10000000 | tf_op jit(solution)/shard_map/weight_terms/pallas_call | solution.py:640
  120.0 5.0 %all-to-all-start = ((bf16[64,152,128]{2,1,0:T(8,128)(2,1)}), bf16[64,152,128]{2,1,0:T(8,128)(2,1)S(1)}, u32[]{:S(2)}, u32[]{:S(2)}) async-start(bf16[64,152,128]{2,1,0:T(8,128)(2,1)} %weight_terms.1), calls=%async_computation | async-start | bytes 4980736 | tf_op jit(solution)/shard_map/all_to_all | solution.py:645
  125.9 30.4 %all-to-all-done.in_ref = bf16[64,152,128]{2,1,0:T(8,128)(2,1)S(1)} async-done(((bf16[64,152,128]{2,1,0:T(8,128)(2,1)}), bf16[64,152,128]{2,1,0:T(8,128)(2,1)S(1)}, u32[]{:S(2)}, u32[]{:S(2)}) %all-to-all-start) | async-done | bytes 2490400 | tf_op jit(solution)/shard_map/all_to_all | solution.py:645
  (52 shorter events, 12.4 us)
Async XLA Ops:
  0.6 4.1 %collective-permute-start = (bf16[144,2,1024]{2,1,0:T(2,128)(2,1)}, bf16[144,2,1024]{2,1,0:T(2,128)(2,1)S(1)}, u32[]{:S(2)}, u32[]{:S(2)}) collective-permute-start(bf16[144,2,1024]{2,1,0:T(2,128)(2,1)} %bitcast.24), channel_id=1, source_target_pairs={{1,0},{3,2},{5,4},{7,6},{9,8},{11,10},{13,12},{15,14},{17,16},{19,... | collective-permute-start | bytes 1769480 | tf_op jit(solution)/shard_map/ppermute | solution.py:548
  19.1 7.9 %collective-permute-start.1 = (bf16[144,1024]{1,0:T(8,128)(2,1)}, bf16[144,1024]{1,0:T(8,128)(2,1)S(1)}, u32[]{:S(2)}, u32[]{:S(2)}) collective-permute-start(bf16[144,1024]{1,0:T(8,128)(2,1)} %get-tuple-element.45), channel_id=1, source_target_pairs={{0,1},{2,3},{4,5},{6,7},{8,9},{10,11},{12,13},{14,15},{16,17},{18,... | collective-permute-start | bytes 884744 | tf_op jit(solution)/shard_map/ppermute | solution.py:556
  20.5 6.6 %collective-permute-start.2 = (bf16[144,1024]{1,0:T(8,128)(2,1)}, bf16[144,1024]{1,0:T(8,128)(2,1)S(1)}, u32[]{:S(2)}, u32[]{:S(2)}) collective-permute-start(bf16[144,1024]{1,0:T(8,128)(2,1)} %get-tuple-element.46), channel_id=1, source_target_pairs={{0,3},{2,1},{4,7},{6,5},{8,11},{10,9},{12,15},{14,13},{16,19},{18,... | collective-permute-start | bytes 884744 | tf_op jit(solution)/shard_map/ppermute | solution.py:556
  21.8 8.5 %collective-permute-start.3 = (bf16[144,1024]{1,0:T(8,128)(2,1)}, bf16[144,1024]{1,0:T(8,128)(2,1)S(1)}, u32[]{:S(2)}, u32[]{:S(2)}) collective-permute-start(bf16[144,1024]{1,0:T(8,128)(2,1)} %get-tuple-element.47), channel_id=1, source_target_pairs={{0,125},{2,127},{4,1},{6,3},{8,5},{10,7},{12,9},{14,11},{16,13},{1... | collective-permute-start | bytes 884744 | tf_op jit(solution)/shard_map/ppermute | solution.py:556
  25.7 7.9 %collective-permute-start.4 = (bf16[144,1024]{1,0:T(8,128)(2,1)}, bf16[144,1024]{1,0:T(8,128)(2,1)S(1)}, u32[]{:S(2)}, u32[]{:S(2)}) collective-permute-start(bf16[144,1024]{1,0:T(8,128)(2,1)} %get-tuple-element.48), channel_id=1, source_target_pairs={{0,127},{2,125},{4,3},{6,1},{8,7},{10,5},{12,11},{14,9},{16,15},{1... | collective-permute-start | bytes 884744 | tf_op jit(solution)/shard_map/ppermute | solution.py:556
  27.0 6.6 %copy-start.13 = (bf16[144,1024]{1,0:T(8,128)(2,1)}, bf16[144,1024]{1,0:T(8,128)(2,1)S(1)}, u32[]{:S(2)}) copy-start(bf16[144,1024]{1,0:T(8,128)(2,1)S(1)} %collective-permute-done.1.r0) | copy-start | bytes 884740
  27.1 6.6 %copy-start.14 = (bf16[144,1024]{1,0:T(8,128)(2,1)}, bf16[144,1024]{1,0:T(8,128)(2,1)S(1)}, u32[]{:S(2)}) copy-start(bf16[144,1024]{1,0:T(8,128)(2,1)S(1)} %collective-permute-done.2.r1) | copy-start | bytes 884740
  30.3 3.4 %copy-start.15 = (bf16[144,1024]{1,0:T(8,128)(2,1)}, bf16[144,1024]{1,0:T(8,128)(2,1)S(1)}, u32[]{:S(2)}) copy-start(bf16[144,1024]{1,0:T(8,128)(2,1)S(1)} %collective-permute-done.3.r2) | copy-start | bytes 884740
  39.5 32.5 %collective-permute-start.5 = (bf16[144,1024]{1,0:T(8,128)(2,1)}, bf16[144,1024]{1,0:T(8,128)(2,1)S(1)}, u32[]{:S(2)}, u32[]{:S(2)}) collective-permute-start(bf16[144,1024]{1,0:T(8,128)(2,1)} %get-tuple-element.52), channel_id=1, source_target_pairs={{1,6},{3,4},{5,10},{7,8},{9,14},{11,12},{13,18},{15,16},{17,22},{1... | collective-permute-start | bytes 884744 | tf_op jit(solution)/shard_map/ppermute | solution.py:562
  40.8 31.2 %collective-permute-start.6 = (bf16[144,1024]{1,0:T(8,128)(2,1)}, bf16[144,1024]{1,0:T(8,128)(2,1)S(1)}, u32[]{:S(2)}, u32[]{:S(2)}) collective-permute-start(bf16[144,1024]{1,0:T(8,128)(2,1)} %get-tuple-element.53), channel_id=1, source_target_pairs={{1,4},{3,6},{5,8},{7,10},{9,12},{11,14},{13,16},{15,18},{17,20},{1... | collective-permute-start | bytes 884744 | tf_op jit(solution)/shard_map/ppermute | solution.py:562
  42.1 29.9 %collective-permute-start.7 = (bf16[144,1024]{1,0:T(8,128)(2,1)}, bf16[144,1024]{1,0:T(8,128)(2,1)S(1)}, u32[]{:S(2)}, u32[]{:S(2)}) collective-permute-start(bf16[144,1024]{1,0:T(8,128)(2,1)} %get-tuple-element.54), channel_id=1, source_target_pairs={{1,2},{3,0},{5,6},{7,4},{9,10},{11,8},{13,14},{15,12},{17,18},{19,... | collective-permute-start | bytes 884744 | tf_op jit(solution)/shard_map/ppermute | solution.py:562
  43.4 28.6 %collective-permute-start.8 = (bf16[144,1024]{1,0:T(8,128)(2,1)}, bf16[144,1024]{1,0:T(8,128)(2,1)S(1)}, u32[]{:S(2)}, u32[]{:S(2)}) collective-permute-start(bf16[144,1024]{1,0:T(8,128)(2,1)} %get-tuple-element.55), channel_id=1, source_target_pairs={{1,0},{3,2},{5,4},{7,6},{9,8},{11,10},{13,12},{15,14},{17,16},{19,... | collective-permute-start | bytes 884744 | tf_op jit(solution)/shard_map/ppermute | solution.py:562
  72.0 22.7 %collective-permute-start.10 = (bf16[288,2048]{1,0:T(8,128)(2,1)}, bf16[288,2048]{1,0:T(8,128)(2,1)S(1)}, u32[]{:S(2)}, u32[]{:S(2)}) collective-permute-start(bf16[288,2048]{1,0:T(8,128)(2,1)} %get-tuple-element.74.n0), channel_id=1, source_target_pairs={{0,8},{4,12},{8,0},{12,4},{32,40},{36,44},{40,32},{44,36},{64,72},... | collective-permute-start | bytes 3538952 | tf_op jit(solution)/shard_map/ppermute | solution.py:579
  72.3 29.6 %collective-permute-start.11 = (bf16[288,2048]{1,0:T(8,128)(2,1)}, bf16[288,2048]{1,0:T(8,128)(2,1)S(1)}, u32[]{:S(2)}, u32[]{:S(2)}) collective-permute-start(bf16[288,2048]{1,0:T(8,128)(2,1)} %get-tuple-element.74.n0), channel_id=1, source_target_pairs={{0,12},{4,0},{8,4},{12,8},{32,44},{36,32},{40,36},{44,40},{64,76},... | collective-permute-start | bytes 3538952 | tf_op jit(solution)/shard_map/ppermute | solution.py:579
  72.4 31.8 %collective-permute-start.9 = (bf16[288,2048]{1,0:T(8,128)(2,1)}, bf16[288,2048]{1,0:T(8,128)(2,1)S(1)}, u32[]{:S(2)}, u32[]{:S(2)}) collective-permute-start(bf16[288,2048]{1,0:T(8,128)(2,1)} %get-tuple-element.74.n0), channel_id=1, source_target_pairs={{0,4},{4,8},{8,12},{12,0},{32,36},{36,40},{40,44},{44,32},{64,68},... | collective-permute-start | bytes 3538952 | tf_op jit(solution)/shard_map/ppermute | solution.py:579
  74.4 22.8 %copy-start.2 = (bf16[4,288,144]{2,1,0:T(8,128)(2,1)S(1)}, bf16[4,288,144]{2,1,0:T(8,128)(2,1)}, u32[]{:S(2)}) copy-start(bf16[4,288,144]{2,1,0:T(8,128)(2,1)} %constant.24.clone.lower_ref) | copy-start | bytes 995332
  91.0 13.1 %copy-start = (bf16[288,2048]{1,0:T(8,128)(2,1)S(1)}, bf16[288,2048]{1,0:T(8,128)(2,1)}, u32[]{:S(2)}) copy-start(bf16[288,2048]{1,0:T(8,128)(2,1)} %get-tuple-element.74.n0) | copy-start | bytes 3538948
  91.1 18.4 %collective-permute-start.12 = (bf16[304,1024]{1,0:T(8,128)(2,1)}, bf16[304,1024]{1,0:T(8,128)(2,1)S(1)}, u32[]{:S(2)}, u32[]{:S(2)}) collective-permute-start(bf16[304,1024]{1,0:T(8,128)(2,1)} %get-tuple-element.76), channel_id=1, source_target_pairs={{0,4},{4,8},{8,12},{12,0},{32,36},{36,40},{40,44},{44,32},{64,68},... | collective-permute-start | bytes 1867784 | tf_op jit(solution)/shard_map/ppermute | solution.py:579
  92.5 23.7 %collective-permute-start.13 = (bf16[304,1024]{1,0:T(8,128)(2,1)}, bf16[304,1024]{1,0:T(8,128)(2,1)S(1)}, u32[]{:S(2)}, u32[]{:S(2)}) collective-permute-start(bf16[304,1024]{1,0:T(8,128)(2,1)} %get-tuple-element.77), channel_id=1, source_target_pairs={{0,8},{4,12},{8,0},{12,4},{32,40},{36,44},{40,32},{44,36},{64,72},... | collective-permute-start | bytes 1867784 | tf_op jit(solution)/shard_map/ppermute | solution.py:579
  94.7 21.5 %collective-permute-start.14 = (bf16[304,1024]{1,0:T(8,128)(2,1)}, bf16[304,1024]{1,0:T(8,128)(2,1)S(1)}, u32[]{:S(2)}, u32[]{:S(2)}) collective-permute-start(bf16[304,1024]{1,0:T(8,128)(2,1)} %get-tuple-element.78), channel_id=1, source_target_pairs={{0,12},{4,0},{8,4},{12,8},{32,44},{36,32},{40,36},{44,40},{64,76},... | collective-permute-start | bytes 1867784 | tf_op jit(solution)/shard_map/ppermute | solution.py:579
  101.8 14.4 %copy-start.1 = (bf16[304,1024]{1,0:T(8,128)(2,1)S(1)}, bf16[304,1024]{1,0:T(8,128)(2,1)}, u32[]{:S(2)}) copy-start(bf16[304,1024]{1,0:T(8,128)(2,1)} %get-tuple-element.75.l0) | copy-start | bytes 1867780
  101.9 18.1 %collective-permute-start.15 = (bf16[144,2,1024]{2,1,0:T(2,128)(2,1)S(1)}, bf16[144,2,1024]{2,1,0:T(2,128)(2,1)}, u32[]{:S(2)}, u32[]{:S(2)}) collective-permute-start(bf16[144,2,1024]{2,1,0:T(2,128)(2,1)S(1)} %second_result.1), channel_id=1, source_target_pairs={{0,1},{2,3},{4,5},{6,7},{8,9},{10,11},{12,13},{14,15},{16,17},{18,... | collective-permute-start | bytes 1769480 | tf_op jit(solution)/shard_map/ppermute | solution.py:548
  120.0 5.0 %copy-start.11 = (bf16[144,2,1024]{2,1,0:T(2,128)(2,1)S(1)}, bf16[144,2,1024]{2,1,0:T(2,128)(2,1)}, u32[]{:S(2)}) copy-start(bf16[144,2,1024]{2,1,0:T(2,128)(2,1)} %get-tuple-element.73) | copy-start | bytes 1769476
  120.0 36.3 %all-to-all-start = ((bf16[64,152,128]{2,1,0:T(8,128)(2,1)}), bf16[64,152,128]{2,1,0:T(8,128)(2,1)S(1)}, u32[]{:S(2)}, u32[]{:S(2)}) async-start(bf16[64,152,128]{2,1,0:T(8,128)(2,1)} %weight_terms.1), calls=%async_computation | async-start | bytes 4980736 | tf_op jit(solution)/shard_map/all_to_all | solution.py:645
  (10 other events, 15.2 us)
where the time goes:
time: 158 us; the launch traced here: 157 us
  waiting for transfers between devices  75.9 us (48%)
  Pallas kernels  43.5 us (28%)
  starting transfers between devices  30.1 us (19%)
  local copies, waits for them, and re-layouts  5.42 us (3%)
    all_to_all x1, waiting for transfers between devices, per_device(): terms = lax.all_to_all(terms, ('lat', 'lon'), 0, 0, tiled=True)  30.4 us
    ppermute x4, waiting for transfers between devices, back(): lax.ppermute(pieces[dl * 2 + dn], axes, roll_pairs(dl, dn, 1))  27.3 us
    pallas_call x1, Pallas kernels, per_device(): call(first_backward_body, 'first_backward', late_shape + [block], [VMEM]...  16.6 us
    pallas_call x1, Pallas kernels, per_device(): call(first_forward_body, 'first_forward', [f32(HEADS * WT, WT), whole, wh...  13.6 us
    ppermute x6, waiting for transfers between devices, deal(): lax.ppermute(values[step], axes, [(g[m], g[(m + step) % GROUP]) for g in...  9.42 us
    ppermute x6, starting transfers between devices, deal(): lax.ppermute(values[step], axes, [(g[m], g[(m + step) % GROUP]) for g in...  8.54 us
    ppermute x4, starting transfers between devices, forth(): got[dl * 2 + dn] = lax.ppermute(piece, axes, roll_pairs(-dl, -dn, 0))  7.84 us
    ppermute x4, waiting for transfers between devices, forth(): got[dl * 2 + dn] = lax.ppermute(piece, axes, roll_pairs(-dl, -dn, 0))  6.57 us
  transfers between devices with their start and end apart: 17, of which 7 were waited for; matrix products, arithmetic and copies ran while one was open for 1% of the time, Pallas kernels for 15%

commit v1 on v0

--- a/solution.py
+++ b/solution.py
@@ -235,23 +235,23 @@
     return jnp.where(lax.axis_index("section") == 0, lax.rem(lat, GROUP), lax.div(lat, 2 * GROUP))
 
 
-def backward_core(xs, go, win, wout, c_ref, proj_ref, e_ref, inv_ref, oh_ref, gctx, gp, bacc, edge, terms, out,
-                  weights, ready, late_ref, late_sem):
+def backward_attention(go, wout, c_ref, proj_ref, e_ref, inv_ref, oh_ref, gctx, gp, bacc, edge, terms,
+                       ready, ready_pair, late_ref, late_sem):
     sent = []
     depth = ring_depth()
     part = [lax.rem(depth + step, GROUP) for step in range(GROUP)]
     for step in range(GROUP):
         cols = pl.ds(pl.multiple_of(256 * part[step], 128), 256)
         sent.append(begin(go.at[:, cols], late_ref[step].at[pl.ds(0, TOK), pl.ds(768, 256)], late_sem.at[step, 0]))
-    if weights:
-        weights[6].wait()
+    ready(0)
     for c in range(0, D, 256):
         gctx[:, c : c + 256] = dot_nt(go[...], wout[c : c + 256, :]).astype(BF)
     edge[...] = jnp.zeros_like(edge)
-    ready()
+    ready(1)
 
     @pl.loop(0, PAIRS, unroll=4)
     def _(p):
+        ready_pair(p)
         eighth = head_masks(0.125)
         ones = head_masks(1.0)
         full = jnp.ones((WT, 128), BF)
@@ -309,9 +309,10 @@
     for step in range(GROUP):
         sent.append(begin(terms, late_ref[step].at[pl.ds(TOK, BIAS_ROWS), :], late_sem.at[step, 2]))
 
-    if weights:
-        for i in range(6):
-            weights[i].wait()
+    return sent
+
+
+def backward_input(xs, go, win, gp, out):
     for c in range(0, D, 256):
         out[:, c : c + 256] = dot_nt(gp[...], win[c : c + 256, :]).astype(BF).astype(F32)
     for at in range(0, TOK, 48):
@@ -327,11 +328,10 @@
         level = jnp.mean(dn, axis=-1, keepdims=True)
         dx = (scale * (dn - level - n * along)).astype(BF).astype(F32)
         out[rows, :] = go[rows, :].astype(F32) + dx
-    return sent
-
-
-def first_forward_body(kind, x_ref, cot_ref, table_ref, oht_ref, rdiff, cdiff, pick_ref, win, wout,
-                       bias_out, n_out, c_out, proj_out, e_out, inv_out, p0, p1, p2, p3,
+
+
+def first_forward_body(kind, x_ref, table_ref, oht_ref, rdiff, cdiff, win, wout,
+                       bias_out, n_out, c_out, proj_out, e_out, inv_out, first_out,
                        win_v, wout_v, bias_v, n, c, proj, e, inv, xs, out, tab, tops, mids, lows, tall, edge, wsem, osem):
     @pl.when(lax.axis_index("section") == 0)
     def _():
@@ -360,18 +360,24 @@
                 sent.append(begin(inv, inv_out, osem.at[5]))
 
         forward_core(xs, win_v, wout_v, bias_v, n, c, proj, e, inv, out, weights, lambda: None, made)
-        load_block(cot_ref, xs)
-        extract(out[...].astype(BF), xs[...].astype(BF), pick_ref, (p0, p1, p2, p3))
+        first_out[...] = out[...].astype(BF)
         for one in sent:
             one.wait()
 
     bias_copy.wait()
+
+
+def pack_body(first_ref, cot_ref, pick_ref, p0, p1, p2, p3, xs):
+    @pl.when(lax.axis_index("section") == 0)
+    def _():
+        load_block(cot_ref, xs)
+        extract(first_ref[...], xs[...].astype(BF), pick_ref, (p0, p1, p2, p3))
 
 
 def second_body(r0, r1, r2, r3, pick_ref, upper_ref, lower_ref, oh_ref, na_ref, ca_ref, bias_ref, win, wout,
                 nc_out, l0, l1, l2, l3, g0, g1, g2, g3,
                 win_v, wout_v, c, proj, e, inv, xs, out, go, gctx, gp, bacc, edge, terms,
-                wsem, isem, lsem, n, bias_v, second):
+                wsem, isem, lsem, n, bias_v, second, psem):
     @pl.when(lax.axis_index("section") == 1)
     def _():
         weights = begin_weights(win, wout, win_v, wout_v, wsem)
@@ -381,15 +387,16 @@
 
         def made(name):
             if name == "n":
-                sent.append(begin(n, nc_out.at[:, pl.ds(0, D)], isem.at[1]))
+                sent.extend(begin(n, nc_out.at[j, :, pl.ds(0, D)], psem.at[j, 0]) for j in range(GROUP))
             if name == "c":
-                sent.append(begin(c, nc_out.at[:, pl.ds(D, D)], isem.at[2]))
+                sent.extend(begin(c, nc_out.at[j, :, pl.ds(D, D)], psem.at[j, 1]) for j in range(GROUP))
 
         forward_core(xs, win_v, wout_v, bias_v, n, c, proj, e, inv, out, weights, bias_copy.wait, made)
         second[...] = out[...].astype(BF)
         go[...] = insert((r0, r1, r2, r3), lower_ref).astype(BF)
-        sent += backward_core(xs, go, win_v, wout_v, c, proj, e, inv, oh_ref, gctx, gp, bacc, edge, terms,
-                              out, None, lambda: None, (l0, l1, l2, l3), lsem)
+        sent += backward_attention(go, wout_v, c, proj, e, inv, oh_ref, gctx, gp, bacc, edge, terms,
+                                   lambda stage: None, lambda p: None, (l0, l1, l2, l3), lsem)
+        backward_input(xs, go, win_v, gp, out)
         extract(out[...].astype(BF), second[...], pick_ref, (g0, g1, g2, g3))
         for one in sent:
             one.wait()
@@ -398,40 +405,44 @@
     def _():
         came = [begin(na_ref, n, isem.at[0]), begin(ca_ref, c, isem.at[1])]
         came[0].wait()
-        gone = begin(n, nc_out.at[:, pl.ds(0, D)], isem.at[2])
+        gone = [begin(n, nc_out.at[j, :, pl.ds(0, D)], psem.at[j, 0]) for j in range(GROUP)]
         came[1].wait()
-        begin(c, nc_out.at[:, pl.ds(D, D)], isem.at[3]).wait()
-        gone.wait()
-
-
-def first_backward_body(x_ref, g0, g1, g2, g3, upper_ref, oh_ref,
-                        ca_ref, proj_ref, e_ref, inv_ref, win, wout, b0, b1, b2, b3,
-                        l0, l1, l2, l3, out_ref,
-                        win_v, wout_v, c, proj, e, inv, xs, out, go, gctx, gp, bacc, edge, terms,
-                        wsem, isem, lsem, hold):
-    @pl.when(lax.axis_index("section") == 0)
-    def _():
-        weights = [None] * 7
-        weights[6] = begin(wout, wout_v, wsem.at[6])
-        copies = [
-            begin(proj_ref, proj, isem.at[0]),
-            begin(e_ref, e, isem.at[1]),
-            begin(inv_ref, inv, isem.at[2]),
-            begin(ca_ref, c, isem.at[3]),
-        ]
-        for i in range(6):
-            cols = pl.ds(512 * i, 512)
-            weights[i] = begin(win.at[:, cols], win_v.at[:, cols], wsem.at[i])
-        go[...] = insert((g0, g1, g2, g3), upper_ref).astype(BF)
-        load_block(x_ref, xs)
-
-        def ready():
-            for one in copies:
+        gone += [begin(c, nc_out.at[j, :, pl.ds(D, D)], psem.at[j, 1]) for j in range(GROUP)]
+        for one in gone:
+            one.wait()
+
+
+def first_backward_body(g0, g1, g2, g3, upper_ref, oh_ref, c_ref, proj_ref, e_ref, inv_ref, wout, b0, b1, b2, b3,
+                        l0, l1, l2, l3, go_out, gp_out,
+                        wout_v, c, proj, e, inv, go, gctx, gp, bacc, edge, terms, grads, upper, oh, hold,
+                        isem, esem, lsem):
+    @pl.when(lax.axis_index("section") == 0)
+    def _():
+        first = [begin(src, grads.at[q], isem.at[q]) for q, src in enumerate((g0, g1, g2, g3))]
+        first.append(begin(upper_ref, upper, isem.at[4]))
+        outer = begin(wout, wout_v, isem.at[5])
+        rest = [begin(proj_ref, proj, isem.at[6]), begin(c_ref, c, isem.at[7]), begin(inv_ref, inv, isem.at[8])]
+
+        def pair_copy(p):
+            rows = pl.ds(pl.multiple_of(p * 2 * TOK, 16), 2 * TOK)
+            return pltpu.make_async_copy(e_ref.at[rows], e.at[rows], esem.at[p])
+
+        for p in range(PAIRS):
+            pair_copy(p).start()
+        last = begin(oh_ref, oh, isem.at[9])
+        for one in first:
+            one.wait()
+        go[...] = insert([grads.at[q] for q in range(4)], upper).astype(BF)
+        go_copy = begin(go, go_out, isem.at[10])
+
+        def ready(stage):
+            for one in [outer] if stage == 0 else rest:
                 one.wait()
 
-        sent = backward_core(xs, go, win_v, wout_v, c, proj, e, inv, oh_ref, gctx, gp, bacc, edge, terms,
-                             out, weights, ready, (l0, l1, l2, l3), lsem)
-        store_block(out, out_ref)
+        last.wait()
+        sent = backward_attention(go, wout_v, c, proj, e, inv, oh, gctx, gp, bacc, edge, terms,
+                                  ready, lambda p: pair_copy(p).wait(), (l0, l1, l2, l3), lsem)
+        sent += [go_copy, begin(gp, gp_out, isem.at[11])]
         for one in sent:
             one.wait()
 
@@ -446,6 +457,14 @@
             one.wait()
 
 
+def input_grad_body(x_ref, go, gp, win, out_ref, xs, out):
+    @pl.when(lax.axis_index("section") == 0)
+    def _():
+        load_block(x_ref, xs)
+        backward_input(xs, go, win, gp, out)
+        store_block(out, out_ref)
+
+
 def second_result_body(g0, g1, g2, g3, lower_ref, out_ref, xs):
     @pl.when(lax.axis_index("section") == 0)
     def _():
@@ -453,8 +472,9 @@
         store_block(xs, out_ref)
 
 
-def flip_body(n0, n1, n2, n3, out_ref, held, sem):
-    copies = [begin(src, held.at[pl.ds(TOK * j, TOK)], sem.at[j]) for j, src in enumerate((n0, n1, n2, n3))]
+def flip_body(in_ref, out_ref, held, sem):
+    source = [lax.rem(ring_depth() + GROUP - step, GROUP) for step in range(GROUP)]
+    copies = [begin(in_ref.at[source[j]], held.at[pl.ds(TOK * j, TOK)], sem.at[j]) for j in range(GROUP)]
     for one in copies:
         one.wait()
 
@@ -571,9 +591,6 @@
                     made.setdefault(key, []).append(flat((y * 2 + x // 2) * 4 + z, x % 2, sec))
         return [made[key] for key in sorted(made)]
 
-    def gather(value, groups):
-        return deal([value] * GROUP, groups)
-
     def deal(values, groups):
         return [values[0]] + [
             lax.ppermute(values[step], axes, [(g[m], g[(m + step) % GROUP]) for g in groups for m in range(GROUP)])
@@ -604,35 +621,44 @@
         + [vbf(BIAS_ROWS, D), dma(7), dma(4), dma(GROUP, 3)]
     )
 
-    bias, n_a, c_a, proj_a, e_a, inv_a, *pieces = call(
-        first_forward_body, "first_forward", [f32(HEADS * WT, WT), whole, whole, wide, exps, invs] + quarter,
-        [SMEM] + [VMEM] * 7 + [HBM] * 2,
+    cot = cross(x, 1)
+    bias, n_a, c_a, proj_a, e_a, inv_a, first_out = call(
+        first_forward_body, "first_forward", [f32(HEADS * WT, WT), whole, whole, wide, exps, invs, whole],
+        [SMEM] + [VMEM] * 5 + [HBM] * 2,
         weights_v + front_v + [vf32(HEADS, OPAD)] + pieces_v + tall + [dma(7), dma(6)],
-        5_000_000_000, 20_000_000, [HBM] * 6 + [VMEM] * 4,
-    )(kind, x, cross(x, 1), offset_bias[0], onehot_t, jnp.asarray(ROWS_DIFFER), jnp.asarray(COLS_DIFFER), pick, win, wout)
+        5_000_000_000, 20_000_000, [HBM] * 6 + [VMEM],
+    )(kind, x, offset_bias[0], onehot_t, jnp.asarray(ROWS_DIFFER), jnp.asarray(COLS_DIFFER), win, wout)
+    pieces = call(
+        pack_body, "pack", quarter, [VMEM] * 3, [vf32(TOK, D)], 340_000_000, 3_000_000, limit=SMALL,
+    )(first_out, cot, pick)
     received = forth(pieces)
     both, *pieces = call(
-        second_body, "second_both", [shape(TOK, 2 * D)] + late_shape + quarter,
+        second_body, "second_both", [shape(GROUP, TOK, 2 * D)] + late_shape + quarter,
         [VMEM] * 8 + [HBM] * 5,
-        back_v + [vbf(TOK, D), vf32(HEADS * WT, WT), vbf(TOK, D)], 12_000_000_000, 20_000_000, [HBM] * 5 + [VMEM] * 4,
+        back_v + [vbf(TOK, D), vf32(HEADS * WT, WT), vbf(TOK, D), dma(GROUP, 2)], 12_000_000_000, 20_000_000, [HBM] * 5 + [VMEM] * 4,
     )(*received, pick, upper, lower, onehot, n_a, c_a, bias, win, wout)
     late_b, grads = pieces[:4], pieces[4:]
     grads = back(grads)
-    grads, both = lax.optimization_barrier((grads, both))
-    both = gather(both, rings("z", 0) + rings("y", 1))
-
-    *late, grad_in = call(
-        first_backward_body, "first_backward", late_shape + [block],
-        [VMEM] * 7 + [HBM] * 10,
-        back_v + [vbf(GROUP, TOK + BIAS_ROWS, D)], 8_000_000_000, 20_000_000, [HBM] * 4 + [VMEM],
-    )(x, *grads, upper, onehot, c_a, proj_a, e_a, inv_a, win, wout, *late_b)
-    late, grad_in, grads = lax.optimization_barrier((late, grad_in, grads))
+    both = lax.all_to_all(both, axes, 0, 0, axis_index_groups=rings("z", 0) + rings("y", 1), tiled=True)
+
+    *late, go_a, gp_a = call(
+        first_backward_body, "first_backward", late_shape + [whole, wide],
+        [HBM] * 15,
+        [vbf(D, D), vbf(TOK, D), vbf(TOK, 3 * D)] + soft_v + [vbf(TOK, D), vbf(TOK, D), vbf(TOK, 3 * D)] + tall
+        + [vbf(BIAS_ROWS, D), vbf(4, 2 * QT, D), vbf(4, TOK, 2 * QT), vbf(256, 256)]
+        + [vbf(GROUP, TOK + BIAS_ROWS, D), dma(12), dma(PAIRS), dma(GROUP, 3)],
+        30_000_000_000, 20_000_000, [HBM] * 6,
+    )(*grads, upper, onehot, c_a, proj_a, e_a, inv_a, wout, *late_b)
+    late, go_a, gp_a, grads = lax.optimization_barrier((late, go_a, gp_a, grads))
     late = deal(late, rings("z", 0) + rings("y", 1))
 
+    grad_in = call(
+        input_grad_body, "input_grad", block, [VMEM] * 4, [vf32(TOK, D), vf32(TOK, D)], 2_000_000_000, 10_000_000,
+    )(x, go_a, gp_a, win)
     flipped = call(
-        flip_body, "flip", shape(2 * D, GROUP * TOK), [HBM] * 4,
+        flip_body, "flip", shape(2 * D, GROUP * TOK), [HBM],
         [vbf(GROUP * TOK, 2 * D), dma(GROUP)], 10_000_000, 10_000_000, limit=SMALL,
-    )(*both)
+    )(both)
     second_out = call(
         second_result_body, "second_result", block, [VMEM] * 5, [vf32(TOK, D)], 170_000_000, 2_000_000, limit=SMALL,
     )(*grads, lower)

time: 158 us -> 154 us (0.975)
  the two profiles are of different devices: /device:TPU:0 before, /device:TPU:1 now
where the time goes in v1:
time: 154 us; the launch traced here: 153 us
  waiting for transfers between devices  64.7 us (42%)
  Pallas kernels  44.8 us (29%)
  starting transfers between devices  33.8 us (22%)
  local copies, waits for them, and re-layouts  6.61 us (4%)
  other arithmetic  1.94 us (1%)
    all_to_all x1, waiting for transfers between devices, per_device(): terms = lax.all_to_all(terms, ('lat', 'lon'), 0, 0, tiled=True)  24.7 us
    pallas_call x1, Pallas kernels, per_device(): call(second_body, 'second_both', [shape(GROUP, TOK, 2 * D)] + late_shape...  22.2 us
    ppermute x4, waiting for transfers between devices, forth(): got[dl * 2 + dn] = lax.ppermute(piece, axes, roll_pairs(-dl, -dn, 0))  15.1 us
    all_to_all x1, waiting for transfers between devices, per_device(): lax.all_to_all(both, axes, 0, 0, axis_index_groups=rings('z', 0) + rings(...  14 us
    all_to_all x1, starting transfers between devices, per_device(): terms = lax.all_to_all(terms, ('lat', 'lon'), 0, 0, tiled=True)  9.02 us
    ppermute x3, waiting for transfers between devices, deal(): lax.ppermute(values[step], axes, [(g[m], g[(m + step) % GROUP]) for g in...  8.74 us
    unnamed x32, local copies, waits for them, and re-layouts  6.61 us
    pallas_call x1, Pallas kernels, per_device(): call(first_forward_body, 'first_forward', [f32(HEADS * WT, WT), whole, wh...  6.41 us
  transfers between devices with their start and end apart: 15, of which 9 were waited for; matrix products, arithmetic and copies ran while one was open for 1% of the time, Pallas kernels for 14%

profile of v1, /device:TPU:1, one launch (start us, length us, event | category | flops | bytes accessed | tf_op | source)
XLA Modules:
  0.0 153.4 jit_solution(12909020381211291556)
XLA Ops:
  0.6 3.4 %collective-permute-start = (bf16[144,2,1024]{2,1,0:T(2,128)(2,1)}, bf16[144,2,1024]{2,1,0:T(2,128)(2,1)S(1)}, u32[]{:S(2)}, u32[]{:S(2)}) collective-permute-start(bf16[144,2,1024]{2,1,0:T(2,128)(2,1)} %bitcast.20), channel_id=1, source_target_pairs={{1,0},{3,2},{5,4},{7,6},{9,8},{11,10},{13,12},{15,14},{17,16},{19,... | collective-permute-start | bytes 1769480 | tf_op jit(solution)/shard_map/ppermute | solution.py:568
  4.7 6.4 %first_forward.1 = (f32[2304,144]{1,0:T(8,128)}, bf16[288,1024]{1,0:T(8,128)(2,1)}, bf16[288,1024]{1,0:T(8,128)(2,1)}, bf16[288,3072]{1,0:T(8,128)(2,1)}, bf16[4...) custom-call(s32[1]{0:T(128)} %bitcast.15.kind, bf16[144,2,1024]{2,1,0:T(2,128)(2,1)} %bitcast.21, ...), custom_call_target="tpu_custom_call" | custom-call | flops 5000000000 | bytes 20000000 | tf_op jit(solution)/shard_map/first_forward/pallas_call | solution.py:625
  17.4 4.3 %collective-permute-done.1.r0 = bf16[144,1024]{1,0:T(8,128)(2,1)S(1)} collective-permute-done((bf16[144,1024]{1,0:T(8,128)(2,1)S(1)}, bf16[144,1024]{1,0:T(8,128)(2,1)S(1)}, u32[]{:S(2)}, u32[]{:S(2)}) %collective-permute-start.1) | collective-permute-done | bytes 294944 | tf_op jit(solution)/shard_map/ppermute | solution.py:576
  21.7 5.8 %collective-permute-done.2.r1 = bf16[144,1024]{1,0:T(8,128)(2,1)S(1)} collective-permute-done((bf16[144,1024]{1,0:T(8,128)(2,1)S(1)}, bf16[144,1024]{1,0:T(8,128)(2,1)S(1)}, u32[]{:S(2)}, u32[]{:S(2)}) %collective-permute-start.2) | collective-permute-done | bytes 294944 | tf_op jit(solution)/shard_map/ppermute | solution.py:576
  27.5 4.9 %collective-permute-done.3.r2 = bf16[144,1024]{1,0:T(8,128)(2,1)S(1)} collective-permute-done((bf16[144,1024]{1,0:T(8,128)(2,1)S(1)}, bf16[144,1024]{1,0:T(8,128)(2,1)S(1)}, u32[]{:S(2)}, u32[]{:S(2)}) %collective-permute-start.3) | collective-permute-done | bytes 294944 | tf_op jit(solution)/shard_map/ppermute | solution.py:576
  33.2 22.2 %second_both.1 = (bf16[4,288,2048]{2,1,0:T(8,128)(2,1)}, bf16[304,1024]{1,0:T(8,128)(2,1)}, bf16[304,1024]{1,0:T(8,128)(2,1)}, bf16[304,1024]{1,0:T(8,128)(2,1)}...) custom-call(bf16[144,1024]{1,0:T(8,128)(2,1)} %copy-done.12, ...), custom_call_target="tpu_custom_call" | custom-call | flops 12000000000 | bytes 20000000 | tf_op jit(solution)/shard_map/second_both/pallas_call | solution.py:635
  55.5 1.3 collective-permute-start.5
  56.8 1.3 collective-permute-start.6
  58.1 1.3 collective-permute-start.7
  59.4 1.5 collective-permute-start.8
  60.9 5.0 %all-to-all-start = ((bf16[4,288,2048]{2,1,0:T(8,128)(2,1)}), bf16[4,288,2048]{2,1,0:T(8,128)(2,1)}, u32[]{:S(2)}, u32[]{:S(2)}) async-start(bf16[4,288,2048]{2,1,0:T(8,128)(2,1)} %get-tuple-element.70), calls=%async_computation | async-start | bytes 9437184 | tf_op jit(solution)/shard_map/all_to_all | solution.py:642
  66.0 2.2 %collective-permute-done.6.g1 = bf16[144,1024]{1,0:T(8,128)(2,1)S(1)} collective-permute-done((bf16[144,1024]{1,0:T(8,128)(2,1)}, bf16[144,1024]{1,0:T(8,128)(2,1)S(1)}, u32[]{:S(2)}, u32[]{:S(2)}) %collective-permute-start.6) | collective-permute-done | bytes 294944 | tf_op jit(solution)/shard_map/ppermute | solution.py:582
  69.1 2.8 %first_backward.1 = (bf16[304,1024]{1,0:T(8,128)(2,1)}, bf16[304,1024]{1,0:T(8,128)(2,1)}, bf16[304,1024]{1,0:T(8,128)(2,1)}, bf16[304,1024]{1,0:T(8,128)(2,1)},...) custom-call(bf16[144,1024]{1,0:T(8,128)(2,1)} %copy-done.3, bf16[144,1024]{1,0:T(8,128)(2,1)} %copy-done.5, ...), custom_call_target="tpu_custom_call" | custom-call | flops 30000001024 | bytes 20000000 | tf_op jit(solution)/shard_map/first_backward/pallas_call | solution.py:644
  71.9 3.0 %collective-permute-start.10 = (bf16[304,1024]{1,0:T(8,128)(2,1)}, bf16[304,1024]{1,0:T(8,128)(2,1)S(1)}, u32[]{:S(2)}, u32[]{:S(2)}) collective-permute-start(bf16[304,1024]{1,0:T(8,128)(2,1)} %get-tuple-element.73), channel_id=1, source_target_pairs={{0,8},{4,12},{8,0},{12,4},{32,40},{36,44},{40,32},{44,36},{64,72},... | collective-permute-start | bytes 1867784 | tf_op jit(solution)/shard_map/ppermute | solution.py:596
  80.2 1.4 collective-permute-start.12
  81.6 14.0 %all-to-all-done.in_ref = bf16[4,288,2048]{2,1,0:T(8,128)(2,1)} async-done(((bf16[4,288,2048]{2,1,0:T(8,128)(2,1)}), bf16[4,288,2048]{2,1,0:T(8,128)(2,1)}, u32[]{:S(2)}, u32[]{:S(2)}) %all-to-all-start) | async-done | bytes 4718624 | tf_op jit(solution)/shard_map/all_to_all | solution.py:642
  95.7 4.0 %flip.1.nct = bf16[2048,1152]{1,0:T(8,128)(2,1)S(1)} custom-call(bf16[4,288,2048]{2,1,0:T(8,128)(2,1)} %all-to-all-done.in_ref), custom_call_target="tpu_custom_call" | custom-call | flops 10000000 | bytes 10000000 | tf_op jit(solution)/shard_map/flip/pallas_call | solution.py:658
  99.7 2.4 %collective-permute-done.10.l2 = bf16[304,1024]{1,0:T(8,128)(2,1)S(1)} collective-permute-done((bf16[304,1024]{1,0:T(8,128)(2,1)}, bf16[304,1024]{1,0:T(8,128)(2,1)S(1)}, u32[]{:S(2)}, u32[]{:S(2)}) %collective-permute-start.10) | collective-permute-done | bytes 622624 | tf_op jit(solution)/shard_map/ppermute | solution.py:596
  102.1 5.1 %collective-permute-done.11.l3 = bf16[304,1024]{1,0:T(8,128)(2,1)S(1)} collective-permute-done((bf16[304,1024]{1,0:T(8,128)(2,1)}, bf16[304,1024]{1,0:T(8,128)(2,1)S(1)}, u32[]{:S(2)}, u32[]{:S(2)}) %collective-permute-start.11) | collective-permute-done | bytes 622624 | tf_op jit(solution)/shard_map/ppermute | solution.py:596
  108.5 3.8 %weight_terms.1 = bf16[64,152,128]{2,1,0:T(8,128)(2,1)} custom-call(bf16[2048,1152]{1,0:T(8,128)(2,1)S(1)} %flip.1.nct, bf16[304,1024]{1,0:T(8,128)(2,1)S(1)} %copy-done, bf16[304,1024]{1,0:T(8,128)(2,1)S(1)} %collective-permute-done.9.l1, bf16[304,1024]{1,0:T(8,128)(2,1)S(1)} %collective-permute-done.10.l2, bf16[304,1024]{1,0:T(8,128)(2,1)S(1)} %collective-permute-done.11.l3), custom_call_target="tpu_custom_call" | custom-call | flops 2400000000 | bytes 10000000 | tf_op jit(solution)/shard_map/weight_terms/pallas_call | solution.py:666
  112.2 9.0 %all-to-all-start.1 = ((bf16[64,152,128]{2,1,0:T(8,128)(2,1)}), bf16[64,152,128]{2,1,0:T(8,128)(2,1)S(1)}, u32[]{:S(2)}, u32[]{:S(2)}) async-start(bf16[64,152,128]{2,1,0:T(8,128)(2,1)} %weight_terms.1), calls=%async_computation.1 | async-start | bytes 4980736 | tf_op jit(solution)/shard_map/all_to_all | solution.py:671
  121.3 4.5 %input_grad.1 = bf16[144,2,1024]{2,1,0:T(2,128)(2,1)} custom-call(bf16[144,2,1024]{2,1,0:T(2,128)(2,1)} %bitcast.22, bf16[288,1024]{1,0:T(8,128)(2,1)} %get-tuple-element.68.go, bf16[288,3072]{1,0:T(8,128)(2,1)} %get-tuple-element.69.gp, bf16[1024,3072]{1,0:T(8,128)(2,1)} %bitcast.18), custom_call_target="tpu_custom_call" | custom-call | flops 2000000000 | bytes 10000000 | tf_op jit(solution)/shard_map/input_grad/pallas_call | solution.py:655
  125.8 1.9 %broadcast_select_fusion = bf16[36,8,1024]{2,1,0:T(8,128)(2,1)} fusion(bf16[36,8,1024]{2,1,0:T(8,128)(2,1)} %bitcast.19, bf16[36,8,1024]{2,1,0:T(8,128)(2,1)} %bitcast.13, pred[]{:T(512)S(6)} %eq.3), kind=kLoop, calls=%fused_computation | loop fusion | flops 294912 | bytes 1769473 | tf_op jit(solution)/shard_map/jit(_where)/select_n | solution.py:672
  127.7 24.7 %all-to-all-done.1.in_ref = bf16[64,152,128]{2,1,0:T(8,128)(2,1)S(1)} async-done(((bf16[64,152,128]{2,1,0:T(8,128)(2,1)}), bf16[64,152,128]{2,1,0:T(8,128)(2,1)S(1)}, u32[]{:S(2)}, u32[]{:S(2)}) %all-to-all-start.1) | async-done | bytes 2490400 | tf_op jit(solution)/shard_map/all_to_all | solution.py:671
  (48 shorter events, 15.5 us)
Async XLA Ops:
  0.6 10.5 %collective-permute-start = (bf16[144,2,1024]{2,1,0:T(2,128)(2,1)}, bf16[144,2,1024]{2,1,0:T(2,128)(2,1)S(1)}, u32[]{:S(2)}, u32[]{:S(2)}) collective-permute-start(bf16[144,2,1024]{2,1,0:T(2,128)(2,1)} %bitcast.20), channel_id=1, source_target_pairs={{1,0},{3,2},{5,4},{7,6},{9,8},{11,10},{13,12},{15,14},{17,16},{19,... | collective-permute-start | bytes 1769480 | tf_op jit(solution)/shard_map/ppermute | solution.py:568
  4.6 6.4 %copy-start.11 = (bf16[4,72,288]{2,1,0:T(8,128)(2,1)S(1)}, bf16[4,72,288]{2,1,0:T(8,128)(2,1)}, u32[]{:S(2)}) copy-start(bf16[4,72,288]{2,1,0:T(8,128)(2,1)} %constant.22.clone.pick_ref) | copy-start | bytes 497668
  11.1 1.1 copy-start.2
  12.2 9.5 %collective-permute-start.1 = (bf16[144,1024]{1,0:T(8,128)(2,1)S(1)}, bf16[144,1024]{1,0:T(8,128)(2,1)S(1)}, u32[]{:S(2)}, u32[]{:S(2)}) collective-permute-start(bf16[144,1024]{1,0:T(8,128)(2,1)S(1)} %get-tuple-element.44), channel_id=1, source_target_pairs={{0,1},{2,3},{4,5},{6,7},{8,9},{10,11},{12,13},{14,15},{16,17},{18,... | collective-permute-start | bytes 884744 | tf_op jit(solution)/shard_map/ppermute | solution.py:576
  13.5 14.1 %collective-permute-start.2 = (bf16[144,1024]{1,0:T(8,128)(2,1)S(1)}, bf16[144,1024]{1,0:T(8,128)(2,1)S(1)}, u32[]{:S(2)}, u32[]{:S(2)}) collective-permute-start(bf16[144,1024]{1,0:T(8,128)(2,1)S(1)} %get-tuple-element.45), channel_id=1, source_target_pairs={{0,3},{2,1},{4,7},{6,5},{8,11},{10,9},{12,15},{14,13},{16,19},{18,... | collective-permute-start | bytes 884744 | tf_op jit(solution)/shard_map/ppermute | solution.py:576
  14.8 17.7 %collective-permute-start.3 = (bf16[144,1024]{1,0:T(8,128)(2,1)S(1)}, bf16[144,1024]{1,0:T(8,128)(2,1)S(1)}, u32[]{:S(2)}, u32[]{:S(2)}) collective-permute-start(bf16[144,1024]{1,0:T(8,128)(2,1)S(1)} %get-tuple-element.46), channel_id=1, source_target_pairs={{0,125},{2,127},{4,1},{6,3},{8,5},{10,7},{12,9},{14,11},{16,13},{1... | collective-permute-start | bytes 884744 | tf_op jit(solution)/shard_map/ppermute | solution.py:576
  16.1 16.4 %collective-permute-start.4 = (bf16[144,1024]{1,0:T(8,128)(2,1)S(1)}, bf16[144,1024]{1,0:T(8,128)(2,1)S(1)}, u32[]{:S(2)}, u32[]{:S(2)}) collective-permute-start(bf16[144,1024]{1,0:T(8,128)(2,1)S(1)} %get-tuple-element.47), channel_id=1, source_target_pairs={{0,127},{2,125},{4,3},{6,1},{8,7},{10,5},{12,11},{14,9},{16,15},{1... | collective-permute-start | bytes 884744 | tf_op jit(solution)/shard_map/ppermute | solution.py:576
  21.7 10.7 %copy-start.12 = (bf16[144,1024]{1,0:T(8,128)(2,1)}, bf16[144,1024]{1,0:T(8,128)(2,1)S(1)}, u32[]{:S(2)}) copy-start(bf16[144,1024]{1,0:T(8,128)(2,1)S(1)} %collective-permute-done.1.r0) | copy-start | bytes 884740
  27.5 4.9 %copy-start.13 = (bf16[144,1024]{1,0:T(8,128)(2,1)}, bf16[144,1024]{1,0:T(8,128)(2,1)S(1)}, u32[]{:S(2)}) copy-start(bf16[144,1024]{1,0:T(8,128)(2,1)S(1)} %collective-permute-done.2.r1) | copy-start | bytes 884740
  55.5 10.5 %collective-permute-start.5 = (bf16[144,1024]{1,0:T(8,128)(2,1)}, bf16[144,1024]{1,0:T(8,128)(2,1)S(1)}, u32[]{:S(2)}, u32[]{:S(2)}) collective-permute-start(bf16[144,1024]{1,0:T(8,128)(2,1)} %get-tuple-element.51), channel_id=1, source_target_pairs={{1,6},{3,4},{5,10},{7,8},{9,14},{11,12},{13,18},{15,16},{17,22},{1... | collective-permute-start | bytes 884744 | tf_op jit(solution)/shard_map/ppermute | solution.py:582
  56.8 11.4 %collective-permute-start.6 = (bf16[144,1024]{1,0:T(8,128)(2,1)}, bf16[144,1024]{1,0:T(8,128)(2,1)S(1)}, u32[]{:S(2)}, u32[]{:S(2)}) collective-permute-start(bf16[144,1024]{1,0:T(8,128)(2,1)} %get-tuple-element.52), channel_id=1, source_target_pairs={{1,4},{3,6},{5,8},{7,10},{9,12},{11,14},{13,16},{15,18},{17,20},{1... | collective-permute-start | bytes 884744 | tf_op jit(solution)/shard_map/ppermute | solution.py:582
  58.1 10.1 %collective-permute-start.7 = (bf16[144,1024]{1,0:T(8,128)(2,1)}, bf16[144,1024]{1,0:T(8,128)(2,1)S(1)}, u32[]{:S(2)}, u32[]{:S(2)}) collective-permute-start(bf16[144,1024]{1,0:T(8,128)(2,1)} %get-tuple-element.53), channel_id=1, source_target_pairs={{1,2},{3,0},{5,6},{7,4},{9,10},{11,8},{13,14},{15,12},{17,18},{19,... | collective-permute-start | bytes 884744 | tf_op jit(solution)/shard_map/ppermute | solution.py:582
  59.4 8.7 %collective-permute-start.8 = (bf16[144,1024]{1,0:T(8,128)(2,1)}, bf16[144,1024]{1,0:T(8,128)(2,1)S(1)}, u32[]{:S(2)}, u32[]{:S(2)}) collective-permute-start(bf16[144,1024]{1,0:T(8,128)(2,1)} %get-tuple-element.54), channel_id=1, source_target_pairs={{1,0},{3,2},{5,4},{7,6},{9,8},{11,10},{13,12},{15,14},{17,16},{19,... | collective-permute-start | bytes 884744 | tf_op jit(solution)/shard_map/ppermute | solution.py:582
  60.9 34.7 %all-to-all-start = ((bf16[4,288,2048]{2,1,0:T(8,128)(2,1)}), bf16[4,288,2048]{2,1,0:T(8,128)(2,1)}, u32[]{:S(2)}, u32[]{:S(2)}) async-start(bf16[4,288,2048]{2,1,0:T(8,128)(2,1)} %get-tuple-element.70), calls=%async_computation | async-start | bytes 9437184 | tf_op jit(solution)/shard_map/all_to_all | solution.py:642
  65.9 2.2 %copy-start.3 = (bf16[144,1024]{1,0:T(8,128)(2,1)}, bf16[144,1024]{1,0:T(8,128)(2,1)S(1)}, u32[]{:S(2)}) copy-start(bf16[144,1024]{1,0:T(8,128)(2,1)S(1)} %collective-permute-done.5.g0) | copy-start | bytes 884740
  69.1 7.3 %copy-start.1 = (bf16[4,288,144]{2,1,0:T(8,128)(2,1)S(1)}, bf16[4,288,144]{2,1,0:T(8,128)(2,1)}, u32[]{:S(2)}) copy-start(bf16[4,288,144]{2,1,0:T(8,128)(2,1)} %constant.24.clone.lower_ref) | copy-start | bytes 995332
  71.9 30.2 %collective-permute-start.10 = (bf16[304,1024]{1,0:T(8,128)(2,1)}, bf16[304,1024]{1,0:T(8,128)(2,1)S(1)}, u32[]{:S(2)}, u32[]{:S(2)}) collective-permute-start(bf16[304,1024]{1,0:T(8,128)(2,1)} %get-tuple-element.73), channel_id=1, source_target_pairs={{0,8},{4,12},{8,0},{12,4},{32,40},{36,44},{40,32},{44,36},{64,72},... | collective-permute-start | bytes 1867784 | tf_op jit(solution)/shard_map/ppermute | solution.py:596
  74.9 32.3 %collective-permute-start.11 = (bf16[304,1024]{1,0:T(8,128)(2,1)}, bf16[304,1024]{1,0:T(8,128)(2,1)S(1)}, u32[]{:S(2)}, u32[]{:S(2)}) collective-permute-start(bf16[304,1024]{1,0:T(8,128)(2,1)} %get-tuple-element.74), channel_id=1, source_target_pairs={{0,12},{4,0},{8,4},{12,8},{32,44},{36,32},{40,36},{44,40},{64,76},... | collective-permute-start | bytes 1867784 | tf_op jit(solution)/shard_map/ppermute | solution.py:596
  75.7 32.8 %collective-permute-start.9 = (bf16[304,1024]{1,0:T(8,128)(2,1)}, bf16[304,1024]{1,0:T(8,128)(2,1)S(1)}, u32[]{:S(2)}, u32[]{:S(2)}) collective-permute-start(bf16[304,1024]{1,0:T(8,128)(2,1)} %get-tuple-element.72), channel_id=1, source_target_pairs={{0,4},{4,8},{8,12},{12,0},{32,36},{36,40},{40,44},{44,32},{64,68},... | collective-permute-start | bytes 1867784 | tf_op jit(solution)/shard_map/ppermute | solution.py:596
  76.4 1.0 copy-start.4
  77.3 1.0 copy-start.6
  80.2 28.2 %copy-start = (bf16[304,1024]{1,0:T(8,128)(2,1)S(1)}, bf16[304,1024]{1,0:T(8,128)(2,1)}, u32[]{:S(2)}) copy-start(bf16[304,1024]{1,0:T(8,128)(2,1)} %get-tuple-element.71.l0) | copy-start | bytes 1867780
  80.2 32.0 %collective-permute-start.12 = (bf16[144,2,1024]{2,1,0:T(2,128)(2,1)S(1)}, bf16[144,2,1024]{2,1,0:T(2,128)(2,1)}, u32[]{:S(2)}, u32[]{:S(2)}) collective-permute-start(bf16[144,2,1024]{2,1,0:T(2,128)(2,1)S(1)} %second_result.1), channel_id=1, source_target_pairs={{0,1},{2,3},{4,5},{6,7},{8,9},{10,11},{12,13},{14,15},{16,17},{18,... | collective-permute-start | bytes 1769480 | tf_op jit(solution)/shard_map/ppermute | solution.py:568
  112.2 40.2 %all-to-all-start.1 = ((bf16[64,152,128]{2,1,0:T(8,128)(2,1)}), bf16[64,152,128]{2,1,0:T(8,128)(2,1)S(1)}, u32[]{:S(2)}, u32[]{:S(2)}) async-start(bf16[64,152,128]{2,1,0:T(8,128)(2,1)} %weight_terms.1), calls=%async_computation.1 | async-start | bytes 4980736 | tf_op jit(solution)/shard_map/all_to_all | solution.py:671
  (7 other events, 5.9 us)

commit v2 on v1

--- a/solution.py
+++ b/solution.py
@@ -192,7 +192,7 @@
     return pl.ds(pl.multiple_of(p * TOK, 8), TOK)
 
 
-def forward_core(xs, win, wout, bias_ref, n_ref, c_ref, proj_ref, e_ref, inv_ref, out, weights, bias_ready, made):
+def forward_core(xs, win, wout, bias_ref, n_ref, c_ref, proj_ref, e_ref, inv_ref, out, weights, bias_ready, made, made_pair):
     for at in range(0, TOK, 48):
         norm_rows(xs, n_ref, at, 48)
     made("n")
@@ -223,6 +223,7 @@
             inv = 1.0 / both[:, 128:]
             c_ref[rows, pair_lanes(p, 0)] = (both[:, :128] * inv).astype(BF)
             inv_ref[pl.ds(pl.multiple_of((p * 2 + w) * WT, 16), WT), :] = inv.astype(BF)
+        made_pair(p)
 
     made("c")
     weights[6].wait()
@@ -235,7 +236,35 @@
     return jnp.where(lax.axis_index("section") == 0, lax.rem(lat, GROUP), lax.div(lat, 2 * GROUP))
 
 
-def backward_attention(go, wout, c_ref, proj_ref, e_ref, inv_ref, oh_ref, gctx, gp, bacc, edge, terms,
+def fold_bias(bacc, edge, oh_ref, terms, late_ref, late_sem):
+    acc = [jnp.zeros((BIAS_ROWS, 256), F32) for _ in range(3)]
+    blank = jnp.zeros((BIAS_ROWS, 128), F32)
+    for rq in range(6):
+        got = []
+        for lq in range(2):
+            taken = [pl.ds((rq * 12 + cq) * 2 + lq, 16, stride=WT) for cq in range(12)]
+            x = jnp.concatenate(
+                [jnp.concatenate([ref[rows, :] for rows in taken], axis=0) for ref in (bacc, edge)], axis=1
+            )
+            top = x.astype(BF)
+            low = (x - top.astype(F32)).astype(BF)
+            got.append(dot(top, oh_ref[...]) + dot(low, oh_ref[...]))
+        levels = [got[0][:, 128:], got[0][:, :128] + got[1][:, 128:], got[1][:, :128]]
+        for dl in range(3):
+            for cq in range(12):
+                one = jnp.concatenate([levels[dl][cq * 16 : cq * 16 + 16], blank], axis=1)
+                shift = ROW_STEP * rq + cq
+                acc[dl] = acc[dl] + (pltpu.roll(one, shift, 1) if shift else one)
+    folded = jnp.zeros((BIAS_ROWS, OPAD), F32)
+    for dl in range(3):
+        one = jnp.concatenate([acc[dl], jnp.zeros((BIAS_ROWS, OPAD - 256), F32)], axis=1)
+        folded = folded + (pltpu.roll(one, LEVEL_STEP * dl, 1) if dl else one)
+    terms[:, :OPAD] = folded.astype(BF)
+    terms[:, OPAD:] = jnp.zeros((BIAS_ROWS, D - OPAD), BF)
+    return [begin(terms, late_ref[step].at[pl.ds(TOK, BIAS_ROWS), :], late_sem.at[step, 2]) for step in range(GROUP)]
+
+
+def backward_attention(go, wout, c_ref, proj_ref, e_ref, inv_ref, gctx, gp, bacc, edge,
                        ready, ready_pair, late_ref, late_sem):
     sent = []
     depth = ring_depth()
@@ -282,33 +311,6 @@
         cols = pl.ds(pl.multiple_of(768 * part[step], 128), 768)
         sent.append(begin(gp.at[:, cols], late_ref[step].at[pl.ds(0, TOK), pl.ds(0, 768)], late_sem.at[step, 1]))
 
-    acc = [jnp.zeros((BIAS_ROWS, 256), F32) for _ in range(3)]
-    blank = jnp.zeros((BIAS_ROWS, 128), F32)
-    for rq in range(6):
-        got = []
-        for lq in range(2):
-            taken = [pl.ds((rq * 12 + cq) * 2 + lq, 16, stride=WT) for cq in range(12)]
-            x = jnp.concatenate(
-                [jnp.concatenate([ref[rows, :] for rows in taken], axis=0) for ref in (bacc, edge)], axis=1
-            )
-            top = x.astype(BF)
-            low = (x - top.astype(F32)).astype(BF)
-            got.append(dot(top, oh_ref[...]) + dot(low, oh_ref[...]))
-        levels = [got[0][:, 128:], got[0][:, :128] + got[1][:, 128:], got[1][:, :128]]
-        for dl in range(3):
-            for cq in range(12):
-                one = jnp.concatenate([levels[dl][cq * 16 : cq * 16 + 16], blank], axis=1)
-                shift = ROW_STEP * rq + cq
-                acc[dl] = acc[dl] + (pltpu.roll(one, shift, 1) if shift else one)
-    folded = jnp.zeros((BIAS_ROWS, OPAD), F32)
-    for dl in range(3):
-        one = jnp.concatenate([acc[dl], jnp.zeros((BIAS_ROWS, OPAD - 256), F32)], axis=1)
-        folded = folded + (pltpu.roll(one, LEVEL_STEP * dl, 1) if dl else one)
-    terms[:, :OPAD] = folded.astype(BF)
-    terms[:, OPAD:] = jnp.zeros((BIAS_ROWS, D - OPAD), BF)
-    for step in range(GROUP):
-        sent.append(begin(terms, late_ref[step].at[pl.ds(TOK, BIAS_ROWS), :], late_sem.at[step, 2]))
-
     return sent
 
 
@@ -332,7 +334,7 @@
 
 def first_forward_body(kind, x_ref, table_ref, oht_ref, rdiff, cdiff, win, wout,
                        bias_out, n_out, c_out, proj_out, e_out, inv_out, first_out,
-                       win_v, wout_v, bias_v, n, c, proj, e, inv, xs, out, tab, tops, mids, lows, tall, edge, wsem, osem):
+                       win_v, wout_v, bias_v, n, c, proj, e, inv, xs, out, tab, tops, mids, lows, tall, edge, wsem, osem, esem):
     @pl.when(lax.axis_index("section") == 0)
     def _():
         begin_weights(win, wout, win_v, wout_v, wsem)
@@ -356,11 +358,23 @@
                 sent.append(begin(proj, proj_out, osem.at[1]))
             if name == "c":
                 sent.append(begin(c, c_out, osem.at[2]))
-                sent.append(begin(e, e_out, osem.at[3]))
-                sent.append(begin(inv, inv_out, osem.at[5]))
-
-        forward_core(xs, win_v, wout_v, bias_v, n, c, proj, e, inv, out, weights, lambda: None, made)
+
+        def pair_copies(p):
+            e_rows = pl.ds(pl.multiple_of(p * 2 * TOK, 16), 2 * TOK)
+            inv_rows = pl.ds(pl.multiple_of(p * 2 * WT, 16), 2 * WT)
+            return [
+                pltpu.make_async_copy(e.at[e_rows], e_out.at[e_rows], esem.at[p, 0]),
+                pltpu.make_async_copy(inv.at[inv_rows], inv_out.at[inv_rows], esem.at[p, 1]),
+            ]
+
+        def made_pair(p):
+            for one in pair_copies(p):
+                one.start()
+
+        forward_core(xs, win_v, wout_v, bias_v, n, c, proj, e, inv, out, weights, lambda: None, made, made_pair)
         first_out[...] = out[...].astype(BF)
+        for p in range(PAIRS):
+            sent += pair_copies(p)
         for one in sent:
             one.wait()
 
@@ -374,14 +388,15 @@
         extract(first_ref[...], xs[...].astype(BF), pick_ref, (p0, p1, p2, p3))
 
 
-def second_body(r0, r1, r2, r3, pick_ref, upper_ref, lower_ref, oh_ref, na_ref, ca_ref, bias_ref, win, wout,
-                nc_out, l0, l1, l2, l3, g0, g1, g2, g3,
+def second_body(r0, r1, r2, r3, upper_ref, pick_hbm, lower_hbm, na_ref, ca_ref, bias_ref, win, wout,
+                nc_out, l0, l1, l2, l3, bacc_out, edge_out, g0, g1, g2, g3,
                 win_v, wout_v, c, proj, e, inv, xs, out, go, gctx, gp, bacc, edge, terms,
-                wsem, isem, lsem, n, bias_v, second, psem):
+                wsem, isem, lsem, n, bias_v, second, psem, pick_ref, lower_ref):
     @pl.when(lax.axis_index("section") == 1)
     def _():
         weights = begin_weights(win, wout, win_v, wout_v, wsem)
         bias_copy = begin(bias_ref, bias_v, isem.at[0])
+        maps = [begin(pick_hbm, pick_ref, isem.at[1]), begin(lower_hbm, lower_ref, isem.at[2])]
         xs[...] = insert((r0, r1, r2, r3), upper_ref)
         sent = []
 
@@ -391,11 +406,14 @@
             if name == "c":
                 sent.extend(begin(c, nc_out.at[j, :, pl.ds(D, D)], psem.at[j, 1]) for j in range(GROUP))
 
-        forward_core(xs, win_v, wout_v, bias_v, n, c, proj, e, inv, out, weights, bias_copy.wait, made)
+        forward_core(xs, win_v, wout_v, bias_v, n, c, proj, e, inv, out, weights, bias_copy.wait, made, lambda p: None)
         second[...] = out[...].astype(BF)
+        for one in maps:
+            one.wait()
         go[...] = insert((r0, r1, r2, r3), lower_ref).astype(BF)
-        sent += backward_attention(go, wout_v, c, proj, e, inv, oh_ref, gctx, gp, bacc, edge, terms,
+        sent += backward_attention(go, wout_v, c, proj, e, inv, gctx, gp, bacc, edge,
                                    lambda stage: None, lambda p: None, (l0, l1, l2, l3), lsem)
+        sent += [begin(bacc, bacc_out, lsem.at[0, 2]), begin(edge, edge_out, lsem.at[1, 2])]
         backward_input(xs, go, win_v, gp, out)
         extract(out[...].astype(BF), second[...], pick_ref, (g0, g1, g2, g3))
         for one in sent:
@@ -412,7 +430,7 @@
             one.wait()
 
 
-def first_backward_body(g0, g1, g2, g3, upper_ref, oh_ref, c_ref, proj_ref, e_ref, inv_ref, wout, b0, b1, b2, b3,
+def first_backward_body(g0, g1, g2, g3, upper_ref, oh_ref, c_ref, proj_ref, e_ref, inv_ref, wout, b0, b1, b2, b3, bacc_b, edge_b,
                         l0, l1, l2, l3, go_out, gp_out,
                         wout_v, c, proj, e, inv, go, gctx, gp, bacc, edge, terms, grads, upper, oh, hold,
                         isem, esem, lsem):
@@ -439,21 +457,26 @@
             for one in [outer] if stage == 0 else rest:
                 one.wait()
 
-        last.wait()
-        sent = backward_attention(go, wout_v, c, proj, e, inv, oh, gctx, gp, bacc, edge, terms,
+        sent = backward_attention(go, wout_v, c, proj, e, inv, gctx, gp, bacc, edge,
                                   ready, lambda p: pair_copy(p).wait(), (l0, l1, l2, l3), lsem)
         sent += [go_copy, begin(gp, gp_out, isem.at[11])]
+        last.wait()
+        sent += fold_bias(bacc, edge, oh, terms, (l0, l1, l2, l3), lsem)
         for one in sent:
             one.wait()
 
     @pl.when(lax.axis_index("section") == 1)
     def _():
-        came = [begin(src, hold.at[j], lsem.at[j, 0]) for j, src in enumerate((b0, b1, b2, b3))]
+        body = pl.ds(0, TOK)
+        came = [begin(src.at[body], hold.at[j], lsem.at[j, 0]) for j, src in enumerate((b0, b1, b2, b3))]
+        sums = [begin(bacc_b, bacc, isem.at[0]), begin(edge_b, edge, isem.at[1]), begin(oh_ref, oh, isem.at[2])]
         gone = []
         for j, dst in enumerate((l0, l1, l2, l3)):
             came[j].wait()
-            gone.append(begin(hold.at[j], dst, lsem.at[j, 1]))
-        for one in gone:
+            gone.append(begin(hold.at[j], dst.at[body], lsem.at[j, 1]))
+        for one in sums:
+            one.wait()
+        for one in gone + fold_bias(bacc, edge, oh, terms, (l0, l1, l2, l3), lsem):
             one.wait()
 
 
@@ -625,7 +648,7 @@
     bias, n_a, c_a, proj_a, e_a, inv_a, first_out = call(
         first_forward_body, "first_forward", [f32(HEADS * WT, WT), whole, whole, wide, exps, invs, whole],
         [SMEM] + [VMEM] * 5 + [HBM] * 2,
-        weights_v + front_v + [vf32(HEADS, OPAD)] + pieces_v + tall + [dma(7), dma(6)],
+        weights_v + front_v + [vf32(HEADS, OPAD)] + pieces_v + tall + [dma(7), dma(6), dma(PAIRS, 2)],
         5_000_000_000, 20_000_000, [HBM] * 6 + [VMEM],
     )(kind, x, offset_bias[0], onehot_t, jnp.asarray(ROWS_DIFFER), jnp.asarray(COLS_DIFFER), win, wout)
     pieces = call(
@@ -633,22 +656,23 @@
     )(first_out, cot, pick)
     received = forth(pieces)
     both, *pieces = call(
-        second_body, "second_both", [shape(GROUP, TOK, 2 * D)] + late_shape + quarter,
-        [VMEM] * 8 + [HBM] * 5,
-        back_v + [vbf(TOK, D), vf32(HEADS * WT, WT), vbf(TOK, D), dma(GROUP, 2)], 12_000_000_000, 20_000_000, [HBM] * 5 + [VMEM] * 4,
-    )(*received, pick, upper, lower, onehot, n_a, c_a, bias, win, wout)
-    late_b, grads = pieces[:4], pieces[4:]
+        second_body, "second_both", [shape(GROUP, TOK, 2 * D)] + late_shape + [f32(HEADS * WT, 128)] * 2 + quarter,
+        [VMEM] * 5 + [HBM] * 7,
+        back_v + [vbf(TOK, D), vf32(HEADS * WT, WT), vbf(TOK, D), dma(GROUP, 2), vbf(4, QT, TOK), vbf(4, TOK, 2 * QT)],
+        12_000_000_000, 20_000_000, [HBM] * 7 + [VMEM] * 4,
+    )(*received, upper, pick, lower, n_a, c_a, bias, win, wout)
+    late_b, sums_b, grads = pieces[:4], pieces[4:6], pieces[6:]
     grads = back(grads)
     both = lax.all_to_all(both, axes, 0, 0, axis_index_groups=rings("z", 0) + rings("y", 1), tiled=True)
 
     *late, go_a, gp_a = call(
         first_backward_body, "first_backward", late_shape + [whole, wide],
-        [HBM] * 15,
+        [HBM] * 17,
         [vbf(D, D), vbf(TOK, D), vbf(TOK, 3 * D)] + soft_v + [vbf(TOK, D), vbf(TOK, D), vbf(TOK, 3 * D)] + tall
         + [vbf(BIAS_ROWS, D), vbf(4, 2 * QT, D), vbf(4, TOK, 2 * QT), vbf(256, 256)]
-        + [vbf(GROUP, TOK + BIAS_ROWS, D), dma(12), dma(PAIRS), dma(GROUP, 3)],
+        + [vbf(GROUP, TOK, D), dma(12), dma(PAIRS), dma(GROUP, 3)],
         30_000_000_000, 20_000_000, [HBM] * 6,
-    )(*grads, upper, onehot, c_a, proj_a, e_a, inv_a, wout, *late_b)
+    )(*grads, upper, onehot, c_a, proj_a, e_a, inv_a, wout, *late_b, *sums_b)
     late, go_a, gp_a, grads = lax.optimization_barrier((late, go_a, gp_a, grads))
     late = deal(late, rings("z", 0) + rings("y", 1))
 

time: 154 us -> 150 us (0.974)
  waiting for transfers between devices: 64.7 us -> 59.7 us
    all_to_all x1, waiting for transfers between devices: 14 us -> 11.3 us  [per_device(): lax.all_to_all(both, axes, 0, 0, axis_index_groups=rings('z', 0) + rings(...]
    pallas_call x1, Pallas kernels: 2.84 us -> 5.27 us  [per_device(): call(first_backward_body, 'first_backward', late_shape + [whole, wide], [...]
    all_to_all x1, waiting for transfers between devices: 24.7 us -> 22.7 us  [per_device(): terms = lax.all_to_all(terms, ('lat', 'lon'), 0, 0, tiled=True)]
    pallas_call x1, Pallas kernels: 22.2 us -> 20.4 us  [per_device(): call(second_body, 'second_both', [shape(GROUP, TOK, 2 * D)] + late_shape...]
  transfers between devices with their start and end apart: 15 -> 15, of which waited for: 9 -> 9; matrix products, arithmetic and copies ran while one was open for 1% -> 1% of each run, Pallas kernels for 14% -> 16%
where the time goes in v2:
time: 150 us; the launch traced here: 149 us
  waiting for transfers between devices  59.7 us (40%)
  Pallas kernels  45.6 us (30%)
  starting transfers between devices  33.8 us (23%)
  local copies, waits for them, and re-layouts  6.72 us (4%)
  other arithmetic  1.94 us (1%)
  between operations  1.52 us (1%)
    all_to_all x1, waiting for transfers between devices, per_device(): terms = lax.all_to_all(terms, ('lat', 'lon'), 0, 0, tiled=True)  22.7 us
    pallas_call x1, Pallas kernels, per_device(): call(second_body, 'second_both', [shape(GROUP, TOK, 2 * D)] + late_shape...  20.4 us
    ppermute x4, waiting for transfers between devices, forth(): got[dl * 2 + dn] = lax.ppermute(piece, axes, roll_pairs(-dl, -dn, 0))  14.6 us
    all_to_all x1, waiting for transfers between devices, per_device(): lax.all_to_all(both, axes, 0, 0, axis_index_groups=rings('z', 0) + rings(...  11.3 us
    all_to_all x1, starting transfers between devices, per_device(): terms = lax.all_to_all(terms, ('lat', 'lon'), 0, 0, tiled=True)  9.19 us
    ppermute x3, waiting for transfers between devices, deal(): lax.ppermute(values[step], axes, [(g[m], g[(m + step) % GROUP]) for g in...  8.75 us
    unnamed x32, local copies, waits for them, and re-layouts  6.72 us
    pallas_call x1, Pallas kernels, per_device(): call(first_forward_body, 'first_forward', [f32(HEADS * WT, WT), whole, wh...  6.56 us
  transfers between devices with their start and end apart: 15, of which 9 were waited for; matrix products, arithmetic and copies ran while one was open for 1% of the time, Pallas kernels for 16%

profile of v2, /device:TPU:1, one launch (start us, length us, event | category | flops | bytes accessed | tf_op | source)
XLA Modules:
  0.0 149.3 jit_solution(442733378170838037)
XLA Ops:
  0.6 3.4 %collective-permute-start = (bf16[144,2,1024]{2,1,0:T(2,128)(2,1)}, bf16[144,2,1024]{2,1,0:T(2,128)(2,1)S(1)}, u32[]{:S(2)}, u32[]{:S(2)}) collective-permute-start(bf16[144,2,1024]{2,1,0:T(2,128)(2,1)} %bitcast.20), channel_id=1, source_target_pairs={{1,0},{3,2},{5,4},{7,6},{9,8},{11,10},{13,12},{15,14},{17,16},{19,... | collective-permute-start | bytes 1769480 | tf_op jit(solution)/shard_map/ppermute | solution.py:591
  4.7 6.6 %first_forward.1 = (f32[2304,144]{1,0:T(8,128)}, bf16[288,1024]{1,0:T(8,128)(2,1)}, bf16[288,1024]{1,0:T(8,128)(2,1)}, bf16[288,3072]{1,0:T(8,128)(2,1)}, bf16[4...) custom-call(s32[1]{0:T(128)} %bitcast.15.kind, bf16[144,2,1024]{2,1,0:T(2,128)(2,1)} %bitcast.21, ...), custom_call_target="tpu_custom_call" | custom-call | flops 5000000000 | bytes 20000000 | tf_op jit(solution)/shard_map/first_forward/pallas_call | solution.py:648
  17.5 3.8 %collective-permute-done.1.r0 = bf16[144,1024]{1,0:T(8,128)(2,1)S(1)} collective-permute-done((bf16[144,1024]{1,0:T(8,128)(2,1)S(1)}, bf16[144,1024]{1,0:T(8,128)(2,1)S(1)}, u32[]{:S(2)}, u32[]{:S(2)}) %collective-permute-start.1) | collective-permute-done | bytes 294944 | tf_op jit(solution)/shard_map/ppermute | solution.py:599
  21.4 5.8 %collective-permute-done.2.r1 = bf16[144,1024]{1,0:T(8,128)(2,1)S(1)} collective-permute-done((bf16[144,1024]{1,0:T(8,128)(2,1)S(1)}, bf16[144,1024]{1,0:T(8,128)(2,1)S(1)}, u32[]{:S(2)}, u32[]{:S(2)}) %collective-permute-start.2) | collective-permute-done | bytes 294944 | tf_op jit(solution)/shard_map/ppermute | solution.py:599
  27.2 4.9 %collective-permute-done.3.r2 = bf16[144,1024]{1,0:T(8,128)(2,1)S(1)} collective-permute-done((bf16[144,1024]{1,0:T(8,128)(2,1)S(1)}, bf16[144,1024]{1,0:T(8,128)(2,1)S(1)}, u32[]{:S(2)}, u32[]{:S(2)}) %collective-permute-start.3) | collective-permute-done | bytes 294944 | tf_op jit(solution)/shard_map/ppermute | solution.py:599
  32.9 20.4 %second_both.1 = (bf16[4,288,2048]{2,1,0:T(8,128)(2,1)}, bf16[304,1024]{1,0:T(8,128)(2,1)}, bf16[304,1024]{1,0:T(8,128)(2,1)}, bf16[304,1024]{1,0:T(8,128)(2,1)}...) custom-call(bf16[144,1024]{1,0:T(8,128)(2,1)} %copy-done.12, ...), custom_call_target="tpu_custom_call" | custom-call | flops 12000000000 | bytes 20000000 | tf_op jit(solution)/shard_map/second_both/pallas_call | solution.py:658
  53.3 1.3 collective-permute-start.5
  54.6 1.3 collective-permute-start.6
  56.0 1.3 collective-permute-start.7
  57.3 1.3 collective-permute-start.8
  58.6 5.0 %all-to-all-start = ((bf16[4,288,2048]{2,1,0:T(8,128)(2,1)}), bf16[4,288,2048]{2,1,0:T(8,128)(2,1)}, u32[]{:S(2)}, u32[]{:S(2)}) async-start(bf16[4,288,2048]{2,1,0:T(8,128)(2,1)} %get-tuple-element.74), calls=%async_computation | async-start | bytes 9437184 | tf_op jit(solution)/shard_map/all_to_all | solution.py:666
  63.6 2.4 %collective-permute-done.6.g1 = bf16[144,1024]{1,0:T(8,128)(2,1)S(1)} collective-permute-done((bf16[144,1024]{1,0:T(8,128)(2,1)}, bf16[144,1024]{1,0:T(8,128)(2,1)S(1)}, u32[]{:S(2)}, u32[]{:S(2)}) %collective-permute-start.6) | collective-permute-done | bytes 294944 | tf_op jit(solution)/shard_map/ppermute | solution.py:605
  67.0 5.3 %first_backward.1 = (bf16[304,1024]{1,0:T(8,128)(2,1)}, bf16[304,1024]{1,0:T(8,128)(2,1)}, bf16[304,1024]{1,0:T(8,128)(2,1)}, bf16[304,1024]{1,0:T(8,128)(2,1)},...) custom-call(bf16[144,1024]{1,0:T(8,128)(2,1)} %copy-done.3, bf16[144,1024]{1,0:T(8,128)(2,1)} %copy-done.5, ...), custom_call_target="tpu_custom_call" | custom-call | flops 30000001024 | bytes 20000000 | tf_op jit(solution)/shard_map/first_backward/pallas_call | solution.py:668
  72.3 3.0 %collective-permute-start.10 = (bf16[304,1024]{1,0:T(8,128)(2,1)}, bf16[304,1024]{1,0:T(8,128)(2,1)S(1)}, u32[]{:S(2)}, u32[]{:S(2)}) collective-permute-start(bf16[304,1024]{1,0:T(8,128)(2,1)} %get-tuple-element.77), channel_id=1, source_target_pairs={{0,8},{4,12},{8,0},{12,4},{32,40},{36,44},{40,32},{44,36},{64,72},... | collective-permute-start | bytes 1867784 | tf_op jit(solution)/shard_map/ppermute | solution.py:619
  80.6 1.4 collective-permute-start.12
  82.1 11.3 %all-to-all-done.in_ref = bf16[4,288,2048]{2,1,0:T(8,128)(2,1)} async-done(((bf16[4,288,2048]{2,1,0:T(8,128)(2,1)}), bf16[4,288,2048]{2,1,0:T(8,128)(2,1)}, u32[]{:S(2)}, u32[]{:S(2)}) %all-to-all-start) | async-done | bytes 4718624 | tf_op jit(solution)/shard_map/all_to_all | solution.py:666
  93.3 4.0 %flip.1.nct = bf16[2048,1152]{1,0:T(8,128)(2,1)S(1)} custom-call(bf16[4,288,2048]{2,1,0:T(8,128)(2,1)} %all-to-all-done.in_ref), custom_call_target="tpu_custom_call" | custom-call | flops 10000000 | bytes 10000000 | tf_op jit(solution)/shard_map/flip/pallas_call | solution.py:682
  97.4 2.4 %collective-permute-done.10.l2 = bf16[304,1024]{1,0:T(8,128)(2,1)S(1)} collective-permute-done((bf16[304,1024]{1,0:T(8,128)(2,1)}, bf16[304,1024]{1,0:T(8,128)(2,1)S(1)}, u32[]{:S(2)}, u32[]{:S(2)}) %collective-permute-start.10) | collective-permute-done | bytes 622624 | tf_op jit(solution)/shard_map/ppermute | solution.py:619
  99.8 5.1 %collective-permute-done.11.l3 = bf16[304,1024]{1,0:T(8,128)(2,1)S(1)} collective-permute-done((bf16[304,1024]{1,0:T(8,128)(2,1)}, bf16[304,1024]{1,0:T(8,128)(2,1)S(1)}, u32[]{:S(2)}, u32[]{:S(2)}) %collective-permute-start.11) | collective-permute-done | bytes 622624 | tf_op jit(solution)/shard_map/ppermute | solution.py:619
  106.1 3.8 %weight_terms.1 = bf16[64,152,128]{2,1,0:T(8,128)(2,1)} custom-call(bf16[2048,1152]{1,0:T(8,128)(2,1)S(1)} %flip.1.nct, bf16[304,1024]{1,0:T(8,128)(2,1)S(1)} %copy-done, bf16[304,1024]{1,0:T(8,128)(2,1)S(1)} %collective-permute-done.9.l1, bf16[304,1024]{1,0:T(8,128)(2,1)S(1)} %collective-permute-done.10.l2, bf16[304,1024]{1,0:T(8,128)(2,1)S(1)} %collective-permute-done.11.l3), custom_call_target="tpu_custom_call" | custom-call | flops 2400000000 | bytes 10000000 | tf_op jit(solution)/shard_map/weight_terms/pallas_call | solution.py:690
  109.9 9.2 %all-to-all-start.1 = ((bf16[64,152,128]{2,1,0:T(8,128)(2,1)}), bf16[64,152,128]{2,1,0:T(8,128)(2,1)S(1)}, u32[]{:S(2)}, u32[]{:S(2)}) async-start(bf16[64,152,128]{2,1,0:T(8,128)(2,1)} %weight_terms.1), calls=%async_computation.1 | async-start | bytes 4980736 | tf_op jit(solution)/shard_map/all_to_all | solution.py:695
  119.1 4.5 %input_grad.1 = bf16[144,2,1024]{2,1,0:T(2,128)(2,1)} custom-call(bf16[144,2,1024]{2,1,0:T(2,128)(2,1)} %bitcast.22, bf16[288,1024]{1,0:T(8,128)(2,1)} %get-tuple-element.72.go, bf16[288,3072]{1,0:T(8,128)(2,1)} %get-tuple-element.73.gp, bf16[1024,3072]{1,0:T(8,128)(2,1)} %bitcast.18), custom_call_target="tpu_custom_call" | custom-call | flops 2000000000 | bytes 10000000 | tf_op jit(solution)/shard_map/input_grad/pallas_call | solution.py:679
  123.6 1.9 %broadcast_select_fusion = bf16[36,8,1024]{2,1,0:T(8,128)(2,1)} fusion(bf16[36,8,1024]{2,1,0:T(8,128)(2,1)} %bitcast.19, bf16[36,8,1024]{2,1,0:T(8,128)(2,1)} %bitcast.13, pred[]{:T(512)S(6)} %eq.3), kind=kLoop, calls=%fused_computation | loop fusion | flops 294912 | bytes 1769473 | tf_op jit(solution)/shard_map/jit(_where)/select_n | solution.py:696
  125.6 22.7 %all-to-all-done.1.in_ref = bf16[64,152,128]{2,1,0:T(8,128)(2,1)S(1)} async-done(((bf16[64,152,128]{2,1,0:T(8,128)(2,1)}), bf16[64,152,128]{2,1,0:T(8,128)(2,1)S(1)}, u32[]{:S(2)}, u32[]{:S(2)}) %all-to-all-start.1) | async-done | bytes 2490400 | tf_op jit(solution)/shard_map/all_to_all | solution.py:695
  (48 shorter events, 15.7 us)
Async XLA Ops:
  0.6 10.6 %collective-permute-start = (bf16[144,2,1024]{2,1,0:T(2,128)(2,1)}, bf16[144,2,1024]{2,1,0:T(2,128)(2,1)S(1)}, u32[]{:S(2)}, u32[]{:S(2)}) collective-permute-start(bf16[144,2,1024]{2,1,0:T(2,128)(2,1)} %bitcast.20), channel_id=1, source_target_pairs={{1,0},{3,2},{5,4},{7,6},{9,8},{11,10},{13,12},{15,14},{17,16},{19,... | collective-permute-start | bytes 1769480 | tf_op jit(solution)/shard_map/ppermute | solution.py:591
  4.6 6.6 %copy-start.11 = (bf16[4,72,288]{2,1,0:T(8,128)(2,1)S(1)}, bf16[4,72,288]{2,1,0:T(8,128)(2,1)}, u32[]{:S(2)}) copy-start(bf16[4,72,288]{2,1,0:T(8,128)(2,1)} %constant.22.clone.pick_ref.pick_hbm) | copy-start | bytes 497668
  11.2 1.1 copy-start.2
  12.3 9.0 %collective-permute-start.1 = (bf16[144,1024]{1,0:T(8,128)(2,1)S(1)}, bf16[144,1024]{1,0:T(8,128)(2,1)S(1)}, u32[]{:S(2)}, u32[]{:S(2)}) collective-permute-start(bf16[144,1024]{1,0:T(8,128)(2,1)S(1)} %get-tuple-element.46), channel_id=1, source_target_pairs={{0,1},{2,3},{4,5},{6,7},{8,9},{10,11},{12,13},{14,15},{16,17},{18,... | collective-permute-start | bytes 884744 | tf_op jit(solution)/shard_map/ppermute | solution.py:599
  13.6 13.6 %collective-permute-start.2 = (bf16[144,1024]{1,0:T(8,128)(2,1)S(1)}, bf16[144,1024]{1,0:T(8,128)(2,1)S(1)}, u32[]{:S(2)}, u32[]{:S(2)}) collective-permute-start(bf16[144,1024]{1,0:T(8,128)(2,1)S(1)} %get-tuple-element.47), channel_id=1, source_target_pairs={{0,3},{2,1},{4,7},{6,5},{8,11},{10,9},{12,15},{14,13},{16,19},{18,... | collective-permute-start | bytes 884744 | tf_op jit(solution)/shard_map/ppermute | solution.py:599
  14.9 17.2 %collective-permute-start.3 = (bf16[144,1024]{1,0:T(8,128)(2,1)S(1)}, bf16[144,1024]{1,0:T(8,128)(2,1)S(1)}, u32[]{:S(2)}, u32[]{:S(2)}) collective-permute-start(bf16[144,1024]{1,0:T(8,128)(2,1)S(1)} %get-tuple-element.48), channel_id=1, source_target_pairs={{0,125},{2,127},{4,1},{6,3},{8,5},{10,7},{12,9},{14,11},{16,13},{1... | collective-permute-start | bytes 884744 | tf_op jit(solution)/shard_map/ppermute | solution.py:599
  16.2 15.9 %collective-permute-start.4 = (bf16[144,1024]{1,0:T(8,128)(2,1)S(1)}, bf16[144,1024]{1,0:T(8,128)(2,1)S(1)}, u32[]{:S(2)}, u32[]{:S(2)}) collective-permute-start(bf16[144,1024]{1,0:T(8,128)(2,1)S(1)} %get-tuple-element.49), channel_id=1, source_target_pairs={{0,127},{2,125},{4,3},{6,1},{8,7},{10,5},{12,11},{14,9},{16,15},{1... | collective-permute-start | bytes 884744 | tf_op jit(solution)/shard_map/ppermute | solution.py:599
  21.3 10.7 %copy-start.12 = (bf16[144,1024]{1,0:T(8,128)(2,1)}, bf16[144,1024]{1,0:T(8,128)(2,1)S(1)}, u32[]{:S(2)}) copy-start(bf16[144,1024]{1,0:T(8,128)(2,1)S(1)} %collective-permute-done.1.r0) | copy-start | bytes 884740
  27.2 4.9 %copy-start.13 = (bf16[144,1024]{1,0:T(8,128)(2,1)}, bf16[144,1024]{1,0:T(8,128)(2,1)S(1)}, u32[]{:S(2)}) copy-start(bf16[144,1024]{1,0:T(8,128)(2,1)S(1)} %collective-permute-done.2.r1) | copy-start | bytes 884740
  53.3 10.3 %collective-permute-start.5 = (bf16[144,1024]{1,0:T(8,128)(2,1)}, bf16[144,1024]{1,0:T(8,128)(2,1)S(1)}, u32[]{:S(2)}, u32[]{:S(2)}) collective-permute-start(bf16[144,1024]{1,0:T(8,128)(2,1)} %get-tuple-element.53), channel_id=1, source_target_pairs={{1,6},{3,4},{5,10},{7,8},{9,14},{11,12},{13,18},{15,16},{17,22},{1... | collective-permute-start | bytes 884744 | tf_op jit(solution)/shard_map/ppermute | solution.py:605
  54.6 11.3 %collective-permute-start.6 = (bf16[144,1024]{1,0:T(8,128)(2,1)}, bf16[144,1024]{1,0:T(8,128)(2,1)S(1)}, u32[]{:S(2)}, u32[]{:S(2)}) collective-permute-start(bf16[144,1024]{1,0:T(8,128)(2,1)} %get-tuple-element.54), channel_id=1, source_target_pairs={{1,4},{3,6},{5,8},{7,10},{9,12},{11,14},{13,16},{15,18},{17,20},{1... | collective-permute-start | bytes 884744 | tf_op jit(solution)/shard_map/ppermute | solution.py:605
  56.0 10.0 %collective-permute-start.7 = (bf16[144,1024]{1,0:T(8,128)(2,1)}, bf16[144,1024]{1,0:T(8,128)(2,1)S(1)}, u32[]{:S(2)}, u32[]{:S(2)}) collective-permute-start(bf16[144,1024]{1,0:T(8,128)(2,1)} %get-tuple-element.55), channel_id=1, source_target_pairs={{1,2},{3,0},{5,6},{7,4},{9,10},{11,8},{13,14},{15,12},{17,18},{19,... | collective-permute-start | bytes 884744 | tf_op jit(solution)/shard_map/ppermute | solution.py:605
  57.3 8.7 %collective-permute-start.8 = (bf16[144,1024]{1,0:T(8,128)(2,1)}, bf16[144,1024]{1,0:T(8,128)(2,1)S(1)}, u32[]{:S(2)}, u32[]{:S(2)}) collective-permute-start(bf16[144,1024]{1,0:T(8,128)(2,1)} %get-tuple-element.56), channel_id=1, source_target_pairs={{1,0},{3,2},{5,4},{7,6},{9,8},{11,10},{13,12},{15,14},{17,16},{19,... | collective-permute-start | bytes 884744 | tf_op jit(solution)/shard_map/ppermute | solution.py:605
  58.6 34.7 %all-to-all-start = ((bf16[4,288,2048]{2,1,0:T(8,128)(2,1)}), bf16[4,288,2048]{2,1,0:T(8,128)(2,1)}, u32[]{:S(2)}, u32[]{:S(2)}) async-start(bf16[4,288,2048]{2,1,0:T(8,128)(2,1)} %get-tuple-element.74), calls=%async_computation | async-start | bytes 9437184 | tf_op jit(solution)/shard_map/all_to_all | solution.py:666
  63.6 2.4 %copy-start.3 = (bf16[144,1024]{1,0:T(8,128)(2,1)}, bf16[144,1024]{1,0:T(8,128)(2,1)S(1)}, u32[]{:S(2)}) copy-start(bf16[144,1024]{1,0:T(8,128)(2,1)S(1)} %collective-permute-done.5.g0) | copy-start | bytes 884740
  66.0 1.0 copy-start.9
  67.0 9.8 %copy-start.1 = (bf16[4,288,144]{2,1,0:T(8,128)(2,1)S(1)}, bf16[4,288,144]{2,1,0:T(8,128)(2,1)}, u32[]{:S(2)}) copy-start(bf16[4,288,144]{2,1,0:T(8,128)(2,1)} %constant.24.clone.lower_hbm.lower_ref) | copy-start | bytes 995332
  72.3 27.4 %collective-permute-start.10 = (bf16[304,1024]{1,0:T(8,128)(2,1)}, bf16[304,1024]{1,0:T(8,128)(2,1)S(1)}, u32[]{:S(2)}, u32[]{:S(2)}) collective-permute-start(bf16[304,1024]{1,0:T(8,128)(2,1)} %get-tuple-element.77), channel_id=1, source_target_pairs={{0,8},{4,12},{8,0},{12,4},{32,40},{36,44},{40,32},{44,36},{64,72},... | collective-permute-start | bytes 1867784 | tf_op jit(solution)/shard_map/ppermute | solution.py:619
  75.3 29.5 %collective-permute-start.11 = (bf16[304,1024]{1,0:T(8,128)(2,1)}, bf16[304,1024]{1,0:T(8,128)(2,1)S(1)}, u32[]{:S(2)}, u32[]{:S(2)}) collective-permute-start(bf16[304,1024]{1,0:T(8,128)(2,1)} %get-tuple-element.78), channel_id=1, source_target_pairs={{0,12},{4,0},{8,4},{12,8},{32,44},{36,32},{40,36},{44,40},{64,76},... | collective-permute-start | bytes 1867784 | tf_op jit(solution)/shard_map/ppermute | solution.py:619
  76.1 30.0 %collective-permute-start.9 = (bf16[304,1024]{1,0:T(8,128)(2,1)}, bf16[304,1024]{1,0:T(8,128)(2,1)S(1)}, u32[]{:S(2)}, u32[]{:S(2)}) collective-permute-start(bf16[304,1024]{1,0:T(8,128)(2,1)} %get-tuple-element.76), channel_id=1, source_target_pairs={{0,4},{4,8},{8,12},{12,0},{32,36},{36,40},{40,44},{44,32},{64,68},... | collective-permute-start | bytes 1867784 | tf_op jit(solution)/shard_map/ppermute | solution.py:619
  76.8 1.0 copy-start.4
  80.6 25.5 %copy-start = (bf16[304,1024]{1,0:T(8,128)(2,1)S(1)}, bf16[304,1024]{1,0:T(8,128)(2,1)}, u32[]{:S(2)}) copy-start(bf16[304,1024]{1,0:T(8,128)(2,1)} %get-tuple-element.75.l0) | copy-start | bytes 1867780
  80.6 29.2 %collective-permute-start.12 = (bf16[144,2,1024]{2,1,0:T(2,128)(2,1)S(1)}, bf16[144,2,1024]{2,1,0:T(2,128)(2,1)}, u32[]{:S(2)}, u32[]{:S(2)}) collective-permute-start(bf16[144,2,1024]{2,1,0:T(2,128)(2,1)S(1)} %second_result.1), channel_id=1, source_target_pairs={{0,1},{2,3},{4,5},{6,7},{8,9},{10,11},{12,13},{14,15},{16,17},{18,... | collective-permute-start | bytes 1769480 | tf_op jit(solution)/shard_map/ppermute | solution.py:591
  109.9 38.4 %all-to-all-start.1 = ((bf16[64,152,128]{2,1,0:T(8,128)(2,1)}), bf16[64,152,128]{2,1,0:T(8,128)(2,1)S(1)}, u32[]{:S(2)}, u32[]{:S(2)}) async-start(bf16[64,152,128]{2,1,0:T(8,128)(2,1)} %weight_terms.1), calls=%async_computation.1 | async-start | bytes 4980736 | tf_op jit(solution)/shard_map/all_to_all | solution.py:695
  (7 other events, 6.0 us)
